TPU v7x, 32 devices: a whole 2x2x4 slice. The times are simulated.
32 devices in a mesh: group: 1, path: 32 (over z, y, x, core).
Axes of the slice: x: 2, y: 2, z: 4, core: 2. Of those that a mesh axis runs over, the one named last changes fastest.
Arguments:
- normals: float32 [8, 32, 8192], P(None, None, ('group', 'path')), may hold values from -6 to 6
- start_state: float32 [32, 8192], P(None, ('group', 'path')), may hold values from -0.12 to 0.12
- later_adjoint: float32 [32, 8192], P(None, ('group', 'path')), may hold values from -1.8 to 1.8
- vol: float32 [8], replicated, may hold values from 0.004 to 0.016
- factor_load: float32 [32, 960], replicated, may hold values from -2.1 to 2.1
- knots: float32 [960], replicated, may hold values from 0.01 to 0.05
- spline_jac: float32 [960, 960], replicated
- cashflows: bfloat16 [256, 960], P(('group', 'path')), may hold values from -0.1875 to 0.1875
- trade_set: int32 [256, 1], P(('group', 'path')), may hold values from 0 to 127
- trade_end: int32 [256], P(('group', 'path')), may hold values from 240 to 960
- set_cpty: int32 [128, 1], P('group'), may hold values from 0 to 63
- default_prob: float32 [8, 64], replicated, may hold values from 0.01 to 0.1
- base_value: float32 [8, 128], P(None, 'group'), may hold values from -3 to 3
Outputs:
- knot_grad: float32 [960], P('group')
- alloc: float32 [256], P(('group', 'path'))
- start_adjoint: float32 [32, 8192], P(None, ('group', 'path'))
All inputs are finite; a program needn't handle non-finite values.
Results may differ from a plain program's by a relative error of at most 0.0011.
Values may be sent and summed in bfloat16 or wider, within the bound.
A program may use at most 64 MiB of HBM per device.

v0:
```python
import math

import jax
import jax.numpy as jnp
from jax import lax
from jax.sharding import PartitionSpec as P

MEAN_REV = 0.05
STEP_YEARS = 0.25
HORIZON_YEARS = 30.0
SHARPNESS = 4.0
LOSS_RATE = 0.6


def curve_terms(knots, spline_jac, date_count, knot_count):
    zero_rate = jnp.dot(spline_jac, knots, precision=lax.Precision.HIGHEST)
    knot_index = jnp.arange(knot_count, dtype=jnp.int32)
    date_index = jnp.arange(date_count, dtype=jnp.int32)
    is_alive = 120 * (knot_index[None, :] + 1) > knot_count * (date_index[:, None] + 1)
    maturity = HORIZON_YEARS * (knot_index + 1).astype(jnp.float32) / knot_count
    fixing = STEP_YEARS * (date_index + 1).astype(jnp.float32)
    horizon = jnp.where(is_alive, maturity[None, :] - fixing[:, None], jnp.float32(0.0))
    loading = (1.0 - jnp.exp(-MEAN_REV * horizon)) / MEAN_REV
    discount = jnp.where(is_alive, jnp.exp(-zero_rate[None, :] * horizon), jnp.float32(0.0))
    return (horizon, loading, discount)


def state_path(start_state, vol, normals):
    decay_factor = math.exp(-MEAN_REV * STEP_YEARS)
    state = start_state
    collected = []
    for index in range(normals.shape[0]):
        state = decay_factor * state + vol[index] * normals[index]
        collected.append(state)
    return jnp.stack(collected)


def per_device(
    normals,
    start_state,
    later_adjoint,
    vol,
    factor_load,
    knots,
    spline_jac,
    cashflows,
    trade_set,
    trade_end,
    set_cpty,
    default_prob,
    base_value,
):
    highest = lax.Precision.HIGHEST
    date_count = normals.shape[0]
    knot_count = knots.shape[0]
    set_count = base_value.shape[1]
    paths_all = normals.shape[2] * lax.axis_size("path")
    horizon, loading, discount = curve_terms(knots, spline_jac, date_count, knot_count)
    knot_index = jnp.arange(knot_count, dtype=jnp.int32)
    live_flows = jnp.where(
        knot_index[None, :] < trade_end[:, None], cashflows, jnp.zeros_like(cashflows)
    )
    set_ids = trade_set[:, 0]
    labels = jnp.arange(set_count, dtype=jnp.int32)
    all_flows, all_sets = (
        lax.all_gather(live_flows, "path", axis=0, tiled=True),
        lax.all_gather(set_ids, "path", axis=0, tiled=True),
    )
    member = (labels[:, None] == all_sets[None, :]).astype(jnp.bfloat16)
    net_flows = jnp.dot(member, all_flows, preferred_element_type=jnp.float32).astype(jnp.bfloat16)
    counter = (
        jnp.arange(default_prob.shape[1], dtype=jnp.int32)[:, None] == set_cpty[:, 0][None, :]
    ).astype(jnp.float32)
    weight = LOSS_RATE * jnp.dot(default_prob, counter, precision=highest)
    states = state_path(start_state, vol, normals)
    shift = jnp.einsum("fm,ifp->imp", factor_load, states, precision=highest)
    bond_term = jnp.exp(-loading[:, :, None] * shift)
    feat_exact = discount[:, :, None] * bond_term
    features = feat_exact.astype(jnp.bfloat16)
    values = jnp.einsum("nm,imp->inp", net_flows, features, preferred_element_type=jnp.float32)
    mean_value = lax.psum(jnp.sum(values, axis=2), "path") / paths_all
    shifted = values - mean_value[:, :, None] + base_value[:, :, None]
    slope = weight[:, :, None] * jax.nn.sigmoid(SHARPNESS * shifted)
    mean_slope = lax.psum(jnp.sum(slope, axis=2), "path") / paths_all
    set_adjoint = (slope - mean_slope[:, :, None]).astype(jnp.bfloat16)
    feat_adjoint = jnp.einsum(
        "nm,inp->imp", net_flows, set_adjoint, preferred_element_type=jnp.float32
    )
    state_local = -jnp.einsum(
        "fm,imp->ifp",
        factor_load,
        feat_adjoint * feat_exact * loading[:, :, None],
        precision=highest,
    )
    discount_grad = jnp.sum(feat_adjoint * bond_term, axis=2)
    rate_adjoint = -jnp.sum(discount_grad * discount * horizon, axis=0) / paths_all
    rate_total = lax.psum(rate_adjoint, "path")
    knot_grad = jnp.dot(spline_jac.T, rate_total, precision=highest)
    load_sums = (
        jnp.einsum("inp,imp->nm", set_adjoint, features, preferred_element_type=jnp.float32)
        / paths_all
    )
    set_rows = load_sums[all_sets]
    trade_part = jnp.sum(all_flows.astype(jnp.float32) * set_rows, axis=1)
    alloc = lax.psum_scatter(trade_part, "path", scatter_dimension=0, tiled=True)
    decay_factor = math.exp(-MEAN_REV * STEP_YEARS)
    carried = later_adjoint + state_local[date_count - 1]
    for index in reversed(range(date_count - 1)):
        carried = state_local[index] + decay_factor * carried
    start_adjoint = decay_factor * carried
    return (knot_grad, alloc, start_adjoint)


def solution(mesh):
    in_specs = (
        P(None, None, ("group", "path")),
        P(None, ("group", "path")),
        P(None, ("group", "path")),
        P(),
        P(),
        P(),
        P(),
        P(("group", "path"), None),
        P(("group", "path"), None),
        P(("group", "path")),
        P("group", None),
        P(),
        P(None, "group"),
    )
    out_specs = (P("group"), P(("group", "path")), P(None, ("group", "path")))
    return jax.shard_map(
        per_device, mesh=mesh, in_specs=in_specs, out_specs=out_specs, check_vma=False
    )
```

profile of v0, /device:TPU:0, one launch (start us, length us, event | category | flops | bytes accessed | tf_op | source)
XLA Modules:
  0.0 270.7 jit_solution(15762425865365894682)
XLA Ops:
  0.7 0.8 bitcast_dynamic-update-slice_fusion.8
  1.5 42.0 %all-reduce = s32[256]{0:T(256)S(1)} all-reduce(s32[256]{0:T(256)S(1)} %bitcast_dynamic-update-slice_fusion.8), channel_id=2, replica_groups=mesh['group'=1,'path'=32] {'path'}, use_global_device_ids=true, to_apply=%add | all-reduce | flops 256 | bytes 2048 | tf_op jit(solution)/shard_map/all_gather | solution.py:67
  43.4 0.6 pad_clamp_fusion
  44.0 0.8 fusion.18
  44.9 5.4 %fusion.50 = f32[1,960]{1,0:T(1,128)S(1)} fusion(f32[960,960]{1,0:T(8,128)} %param.19, f32[960,1]{0,1:T(1,128)} %bitcast.192), kind=kOutput, calls=%fused_computation.96 | convolution fusion | flops 11059200 | bytes 3694080 | tf_op jit(solution)/shard_map/dot_general | solution.py:16
  50.4 1.6 fusion.48
  52.0 0.8 fusion.42
  52.8 0.7 subtract_multiply_fusion
  53.5 1.5 bitcast_dynamic-update-slice_fusion.7
  55.0 2.0 bitcast_dynamic-update-slice_fusion.6
  57.0 1.5 bitcast_dynamic-update-slice_fusion.5
  58.5 2.0 bitcast_dynamic-update-slice_fusion.4
  60.5 1.5 bitcast_dynamic-update-slice_fusion.3
  62.0 2.1 bitcast_dynamic-update-slice_fusion.2
  64.1 1.4 bitcast_dynamic-update-slice_fusion.1
  65.5 2.1 bitcast_dynamic-update-slice_fusion
  67.5 41.6 %all_gather.7 = bf16[256,960]{1,0:T(8,128)(2,1)S(1)} all-gather(bf16[8,960]{1,0:T(8,128)(2,1)S(1)} %fusion.42), channel_id=1, replica_groups=mesh['group'=1,'path'=32] {'path'}, dimensions={0}, use_global_device_ids=true | all-gather | bytes 506880 | tf_op jit(solution)/shard_map/all_gather | solution.py:66
  109.2 0.3 fusion.17
  109.5 6.5 %fusion.23 = f32[8,256,960]{1,2,0:T(8,128)S(1)} fusion(f32[8,32,256]{2,1,0:T(8,128)S(1)} %bitcast_dynamic-update-slice_fusion, f32[32,960]{1,0:T(8,128)S(1)} %copy-done), kind=kOutput, calls=%fused_computation.28 | convolution fusion | flops 754974720 | bytes 8249344 | tf_op jit(solution)/shard_map/fm,ifp->imp/dot_general | solution.py:76
  116.0 3.1 %copy-done.1 = f32[8,256,960]{1,2,0:T(8,128)} copy-done((f32[8,256,960]{1,2,0:T(8,128)}, f32[8,256,960]{1,2,0:T(8,128)S(1)}, u32[]{:S(2)}) %copy-start.1) | copy-done | bytes 7864344
  119.1 5.4 %fusion.49 = (f32[8,128]{1,0:T(8,128)S(1)}, f32[8,128,256]{1,2,0:T(8,128)S(1)}) fusion(bf16[128,960,1]{0,1,2:T(8,128)(2,1)S(1)} %fusion.17, f32[8,256,960]{1,2,0:T(8,128)S(1)} %fusion.23, f32[8,960]{1,0:T(8,128)S(1)} %get-tuple-element.12, f32[8,960]{1,0:T(8,128)S(1)} %get-tuple-element.13), kind=kOutput, calls=%fused_computation.95 | convolution fusion | flops 509475840 | bytes 9224192 | tf_op jit(solution)/shard_map/nm,imp->inp/dot_general | solution.py:80
  124.5 37.1 %psum.21 = f32[8,128]{1,0:T(8,128)S(1)} all-reduce(f32[8,128]{1,0:T(8,128)S(1)} %get-tuple-element.22), channel_id=1, replica_groups=mesh['group'=1,'path'=32] {'path'}, use_global_device_ids=true, to_apply=%region_1.2 | all-reduce | flops 1024 | bytes 8192 | tf_op jit(solution)/shard_map/psum | solution.py:81
  162.0 41.2 %psum.22 = f32[8,128]{1,0:T(8,128)S(1)} all-reduce(f32[8,128]{1,0:T(8,128)S(1)} %fusion.47), channel_id=1, replica_groups=mesh['group'=1,'path'=32] {'path'}, use_global_device_ids=true, to_apply=%region_3.4 | all-reduce | flops 1024 | bytes 8192 | tf_op jit(solution)/shard_map/psum | solution.py:84
  203.2 0.6 copy-done.15
  203.8 5.4 %fusion.10 = f32[128,960]{0,1:T(8,128)S(1)} fusion(f32[8,256,960]{1,2,0:T(8,128)} %copy-done.1, f32[8,960]{1,0:T(8,128)S(1)} %get-tuple-element.12, f32[8,960]{1,0:T(8,128)S(1)} %get-tuple-element.13, f32[8,128]{1,0:T(8,128)S(1)} %broadcast_multiply_fusion, f32[8,128,256]{1,2,0:T(8,128)S(1)} %get-tuple-element.23, f32[8,128]{1,0:T(8,128)S(1)} %copy-done.13, ...), kind=kOutput, calls=%fused_computation.16 | convolution fusion | flops 511696896 | bytes 9482240 | tf_op jit(solution)/shard_map/inp,imp->nm/dot_general | solution.py:100
  209.4 1.2 gather_fusion
  210.8 6.4 %fusion = (f32[8,960]{1,0:T(8,128)S(1)}, f32[8,256,960]{1,2,0:T(8,128)S(1)}) fusion(f32[8,256,960]{1,2,0:T(8,128)} %copy-done.1, f32[8,960]{1,0:T(8,128)S(1)} %get-tuple-element.12, bf16[128,960,1]{0,1,2:T(8,128)(2,1)S(1)} %fusion.17, f32[8,128]{1,0:T(8,128)} %copy-done.15, f32[8,128]{1,0:T(8,128)} %param.25, f32[8,128,256]{1,2,0:T(8,128)S(1)} %get-tuple-element.23, ...), kind=kOutput, calls=%fused_computation.3 | convolution fusion | flops 511566336 | bytes 17100800 | tf_op jit(solution)/shard_map/nm,inp->imp/dot_general | solution.py:86
  217.4 7.6 %fusion.14 = f32[8,32,256]{2,1,0:T(8,128)S(1)} fusion(f32[8,256,960]{1,2,0:T(8,128)S(1)} %get-tuple-element.25, f32[8,256,960]{1,2,0:T(8,128)S(1)} %bitcast.190, f32[8,960]{1,0:T(8,128)S(1)} %copy-done.4, f32[8,960]{1,0:T(8,128)S(1)} %get-tuple-element.12, f32[8,960]{1,0:T(8,128)S(1)} %copy-done.3, f32[32,960]{1,0:T(8,128)S(1)} %copy-done), kind=kOutput, calls=%fused_computation.19 | convolution fusion | flops 762904576 | bytes 16205824 | tf_op jit(solution)/shard_map/fm,imp->ifp/dot_general | solution.py:89
  225.0 0.6 fusion.41
  225.8 39.6 %all-reduce.2 = (f32[960]{0:T(1024)S(1)}, f32[256]{0:T(256)S(1)}) all-reduce(f32[960]{0:T(1024)S(1)} %negate_multiply_fusion, f32[256]{0:T(256)S(1)} %multiply_reduce_fusion), channel_id=1, replica_groups=mesh['group'=1,'path'=32] {'path'}, use_global_device_ids=true, to_apply=%region_6.7 | all-reduce | flops 1216 | bytes 9728 | tf_op jit(solution)/shard_map/psum | solution.py:97
  265.4 4.7 %fusion.5 = f32[1,960]{1,0:T(1,128)} fusion(f32[960,1]{0,1:T(1,128)S(1)} %bitcast.194, f32[960,960]{1,0:T(8,128)} %param.19), kind=kOutput, calls=%fused_computation.9 | convolution fusion | flops 11059200 | bytes 3694080 | tf_op jit(solution)/shard_map/dot_general | solution.py:98
  270.1 0.6 dynamic-slice
  (57 shorter events, 1.0 us)
Async XLA Ops:
  0.6 108.9 %copy-start = (f32[32,960]{1,0:T(8,128)S(1)}, f32[32,960]{1,0:T(8,128)}, u32[]{:S(2)}) copy-start(f32[32,960]{1,0:T(8,128)} %param.17) | copy-start | bytes 368644
  0.7 123.8 %copy-start.16 = (s32[8]{0:T(128)}, s32[8]{0:T(128)S(1)}, u32[]{:S(2)}) copy-start(s32[8]{0:T(128)S(1)} %fusion.46) | copy-start | bytes 100
  0.7 123.8 %copy-start.18 = (f32[8]{0:T(128)}, f32[8]{0:T(128)S(1)}, u32[]{:S(2)}) copy-start(f32[8]{0:T(128)S(1)} %convert_multiply_fusion.1) | copy-start | bytes 100
  44.9 158.3 %copy-start.14 = (f32[8,128]{1,0:T(8,128)}, f32[8,128]{1,0:T(8,128)S(1)}, u32[]{:S(2)}) copy-start(f32[8,128]{1,0:T(8,128)S(1)} %fusion.18) | copy-start | bytes 12292
  44.9 79.6 %copy-start.5 = (s32[960]{0:T(1024)}, s32[960]{0:T(1024)S(1)}, u32[]{:S(2)}) copy-start(s32[960]{0:T(1024)S(1)} %fusion.44) | copy-start | bytes 11524
  44.9 79.6 %copy-start.7 = (f32[960]{0:T(1024)}, f32[960]{0:T(1024)S(1)}, u32[]{:S(2)}) copy-start(f32[960]{0:T(1024)S(1)} %convert_multiply_fusion) | copy-start | bytes 11524
  50.4 74.2 %copy-start.9 = (f32[960]{0:T(1024)}, f32[960]{0:T(1024)S(1)}, u32[]{:S(2)}) copy-start(f32[960]{0:T(1024)S(1)} %neg.24) | copy-start | bytes 11524
  53.5 149.7 %copy-start.2 = (f32[8,960]{1,0:T(8,128)}, f32[8,960]{1,0:T(8,128)S(1)}, u32[]{:S(2)}) copy-start(f32[8,960]{1,0:T(8,128)S(1)} %get-tuple-element.13) | copy-start | bytes 92164
  109.5 52.1 %copy-start.13 = (f32[8,128]{1,0:T(8,128)S(1)}, f32[8,128]{1,0:T(8,128)}, u32[]{:S(2)}) copy-start(f32[8,128]{1,0:T(8,128)} %param.25) | copy-start | bytes 12292
  116.0 3.1 %copy-start.1 = (f32[8,256,960]{1,2,0:T(8,128)}, f32[8,256,960]{1,2,0:T(8,128)S(1)}, u32[]{:S(2)}) copy-start(f32[8,256,960]{1,2,0:T(8,128)S(1)} %fusion.23) | copy-start | bytes 23592964
  161.6 41.6 %copy-start.11 = (f32[8,128]{1,0:T(8,128)}, f32[8,128]{1,0:T(8,128)S(1)}, u32[]{:S(2)}) copy-start(f32[8,128]{1,0:T(8,128)S(1)} %broadcast_multiply_fusion.1) | copy-start | bytes 12292
  203.2 0.6 copy-start.15
  210.6 6.7 %slice-start = ((s8[7864320]{0:T(1024)(128)(4,1)}), s8[4194304]{0:T(1024)(128)(4,1)S(1)}, s32[]{:S(2)}) async-start(s8[7864320]{0:T(1024)(128)(4,1)} %bitcast.189), calls=%async_computation | async-start | bytes 8388608
  210.8 6.5 %slice-start.1 = ((s8[7864320]{0:T(1024)(128)(4,1)}), s8[3670016]{0:T(1024)(128)(4,1)S(1)}, s32[]{:S(2)}) async-start(s8[7864320]{0:T(1024)(128)(4,1)} %bitcast.189), calls=%async_computation.1 | async-start | bytes 7340032
  210.8 6.5 %copy-start.3 = (f32[8,960]{1,0:T(8,128)S(1)}, f32[8,960]{1,0:T(8,128)}, u32[]{:S(2)}) copy-start(f32[8,960]{1,0:T(8,128)} %copy-done.2) | copy-start | bytes 92164
  210.8 6.5 %copy-start.4 = (f32[8,960]{1,0:T(8,128)S(1)}, f32[8,960]{1,0:T(8,128)}, u32[]{:S(2)}) copy-start(f32[8,960]{1,0:T(8,128)} %get-tuple-element.11) | copy-start | bytes 92164
  217.3 7.6 %copy-start.12 = (f32[32,256]{1,0:T(8,128)S(1)}, f32[32,256]{1,0:T(8,128)}, u32[]{:S(2)}) copy-start(f32[32,256]{1,0:T(8,128)} %param.15) | copy-start | bytes 98308
  217.3 8.3 %copy-start.6 = (s32[960]{0:T(1024)S(1)}, s32[960]{0:T(1024)}, u32[]{:S(2)}) copy-start(s32[960]{0:T(1024)} %copy-done.5) | copy-start | bytes 11524
  217.4 8.3 %copy-start.8 = (f32[960]{0:T(1024)S(1)}, f32[960]{0:T(1024)}, u32[]{:S(2)}) copy-start(f32[960]{0:T(1024)} %copy-done.7) | copy-start | bytes 11524
  217.4 8.3 %copy-start.10 = (f32[960]{0:T(1024)S(1)}, f32[960]{0:T(1024)}, u32[]{:S(2)}) copy-start(f32[960]{0:T(1024)} %copy-done.9) | copy-start | bytes 11524
  217.4 8.3 %copy-start.17 = (s32[8]{0:T(128)S(1)}, s32[8]{0:T(128)}, u32[]{:S(2)}) copy-start(s32[8]{0:T(128)} %copy-done.16) | copy-start | bytes 100
  217.4 8.3 %copy-start.19 = (f32[8]{0:T(128)S(1)}, f32[8]{0:T(128)}, u32[]{:S(2)}) copy-start(f32[8]{0:T(128)} %copy-done.18) | copy-start | bytes 100
where the time goes:
time: 272 us; the launch traced here: 271 us
  blocking collectives  202 us (74%)
  matrix products  42.6 us (16%)
  other arithmetic  17.4 us (6%)
  local copies, waits for them, and re-layouts  8.13 us (3%)
    all_gather x1, blocking collectives, per_device(): lax.all_gather(set_ids, 'path', axis=0, tiled=True)  42 us
    all_gather x1, blocking collectives, per_device(): lax.all_gather(live_flows, 'path', axis=0, tiled=True)  41.6 us
    psum x1, blocking collectives, per_device(): mean_slope = lax.psum(jnp.sum(slope, axis=2), 'path') / paths_all  41.2 us
    psum x1, blocking collectives, per_device(): rate_total = lax.psum(rate_adjoint, 'path')  39.6 us
    psum x1, blocking collectives, per_device(): mean_value = lax.psum(jnp.sum(values, axis=2), 'path') / paths_all  37.1 us
    unnamed x8, other arithmetic  12 us
    dot_general x1, matrix products, per_device(): jnp.einsum('fm,imp->ifp', factor_load, feat_adjoint * feat_exact * loadin...  7.57 us
    dot_general x1, matrix products, per_device(): shift = jnp.einsum('fm,ifp->imp', factor_load, states, precision=highest)  6.46 us

commit v1 on v0

v1 whole, which is shorter than its diff:
```python
import functools
import math

import jax
import jax.numpy as jnp
from jax import lax
from jax.experimental import pallas as pl
from jax.experimental.pallas import tpu as pltpu
from jax.sharding import PartitionSpec as P

MEAN_REV = 0.05
STEP_YEARS = 0.25
HORIZON_YEARS = 30.0
SHARPNESS = 4.0
LOSS_RATE = 0.6
DECAY = math.exp(-MEAN_REV * STEP_YEARS)
MESH = pl.DeviceIdType.MESH
F32 = jnp.float32
BF16 = jnp.bfloat16


def dot(a, b, dims, precision=None):
    return lax.dot_general(
        a, b, (dims, ((), ())), preferred_element_type=F32, precision=precision
    )


NN = ((1,), (0,))
NT = ((1,), (1,))
TN = ((0,), (0,))


def split3(x):
    high = x.astype(BF16)
    rest = x - high.astype(F32)
    mid = rest.astype(BF16)
    low = (rest - mid.astype(F32)).astype(BF16)
    return high, mid, low


def split2(x):
    high = x.astype(BF16)
    return high, (x - high.astype(F32)).astype(BF16)


def diagonal(rows):
    return lax.broadcasted_iota(jnp.int32, (rows, rows), 0) == lax.broadcasted_iota(
        jnp.int32, (rows, rows), 1
    )


def column_to_row(column):
    count = column.shape[0]
    pieces = []
    for first in range(0, count, 128):
        rows = min(128, count - first)
        piece = jnp.broadcast_to(column[first : first + rows], (rows, rows))
        pieces.append(jnp.sum(jnp.where(diagonal(rows), piece, 0.0), axis=0, keepdims=True))
    return jnp.concatenate(pieces, axis=1) if len(pieces) > 1 else pieces[0]


def row_to_column(row):
    count = row.shape[1]
    pieces = []
    for first in range(0, count, 128):
        rows = min(128, count - first)
        piece = jnp.broadcast_to(row[:, first : first + rows], (rows, rows))
        pieces.append(jnp.sum(jnp.where(diagonal(rows), piece, 0.0), axis=1, keepdims=True))
    return jnp.concatenate(pieces, axis=0) if len(pieces) > 1 else pieces[0]


def kernel(
    n,
    vol,
    trade_end,
    normals,
    start_state,
    later_adjoint,
    factor_load,
    knots,
    spline_hbm,
    cashflows,
    trade_set,
    set_cpty,
    default_prob,
    base_value,
    knot_out,
    alloc_out,
    start_out,
    spline,
    flows,
    value_sums,
    slope_sums,
    rate_sums,
    alloc_sent,
    alloc_sums,
    net,
    exact,
    features,
    values,
    adjoint,
    weighted,
    rate_acc,
    loading_rows,
    discount_rows,
    horizon_rows,
    weight_rows,
    load_split,
    spline_sem,
    send_sems,
    recv_sems,
):
    dates, factors, paths = normals.shape
    grid = knots.shape[1]
    trades = cashflows.shape[0]
    sets = base_value.shape[1]
    half = flows.shape[3] - sets
    chips = n // 2
    paths_all = paths * n
    me = lax.axis_index("path")
    chip, core = me // 2, me % 2
    partner = me + 1 - 2 * core

    spline_copy = pltpu.make_async_copy(spline_hbm, spline, spline_sem)
    spline_copy.start()

    barrier = pltpu.get_barrier_semaphore()

    def greet(step, carry):
        pl.semaphore_signal(
            barrier, inc=1, device_id={"path": lax.rem(me + step, n)}, device_id_type=MESH
        )
        return carry

    lax.fori_loop(1, n, greet, 0)

    end = jnp.zeros((trades, 1), jnp.int32)
    for trade in range(trades):
        at = lax.broadcasted_iota(jnp.int32, (trades, 1), 0) == trade
        end = jnp.where(at, trade_end[trade], end)
    live = jnp.where(
        lax.broadcasted_iota(jnp.int32, (trades, grid), 1) < end,
        cashflows[...].astype(F32),
        0.0,
    )
    upper = jnp.concatenate(
        [live[:, half:], jnp.zeros((trades, 2 * half - grid), F32)], axis=1
    )
    one_hot = (lax.broadcasted_iota(jnp.int32, (trades, sets), 1) == trade_set[...]).astype(F32)
    message = jnp.concatenate(
        [
            jnp.concatenate([live[:, :half], upper], axis=0),
            jnp.concatenate([one_hot, one_hot], axis=0),
        ],
        axis=1,
    )
    flows[core, chip] = message.astype(BF16)

    pl.semaphore_wait(barrier, n - 1)

    def send_flows(step, carry):
        pltpu.make_async_remote_copy(
            src_ref=flows.at[core, chip],
            dst_ref=flows.at[core, chip],
            send_sem=send_sems.at[0],
            recv_sem=recv_sems.at[0],
            device_id={"path": lax.rem(me + 2 * step, n)},
            device_id_type=MESH,
        ).start()
        return carry

    lax.fori_loop(1, chips, send_flows, 0)

    def send_all(buffer, which):
        def send(step, carry):
            pltpu.make_async_remote_copy(
                src_ref=buffer.at[me],
                dst_ref=buffer.at[me],
                send_sem=send_sems.at[which],
                recv_sem=recv_sems.at[which],
                device_id={"path": lax.rem(me + step, n)},
                device_id_type=MESH,
            ).start()
            return carry

        lax.fori_loop(1, n, send, 0)

    def wait_all(buffer, sems, which):
        others = buffer.at[pl.ds(0, n - 1)]
        pltpu.make_async_copy(others, others, sems.at[which]).wait()

    index = lax.broadcasted_iota(jnp.int32, (dates, grid), 1)
    date = lax.broadcasted_iota(jnp.int32, (dates, grid), 0)
    alive = 120 * (index + 1) > grid * (date + 1)
    maturity = HORIZON_YEARS * (index + 1).astype(F32) / grid
    fixing = STEP_YEARS * (date + 1).astype(F32)
    horizon = jnp.where(alive, maturity - fixing, 0.0)
    horizon_rows[...] = horizon
    loading_rows[...] = (1.0 - jnp.exp(-MEAN_REV * horizon)) / MEAN_REV
    spline_copy.wait()
    zero_rate = column_to_row(jnp.sum(spline[...] * knots[...], axis=1, keepdims=True))
    discount_rows[...] = jnp.where(alive, jnp.exp(-zero_rate * horizon), 0.0)

    counter = (
        lax.broadcasted_iota(jnp.int32, (sets, default_prob.shape[1]), 1) == set_cpty[...]
    ).astype(F32)
    weight_rows[...] = LOSS_RATE * dot(
        default_prob[...], counter, NT, precision=lax.Precision.HIGHEST
    )

    high, mid, low = split3(factor_load[...])
    load_split[...] = jnp.concatenate([high, high, mid, high, mid, low], axis=0)

    def forward(i, state):
        state = DECAY * state + vol[i] * normals[i]
        s_high, s_mid, s_low = split3(state)
        stacked = jnp.concatenate([s_high, s_mid, s_high, s_low, s_mid, s_high], axis=0)
        shift = dot(stacked, load_split[...], TN)
        bond = jnp.exp(-(loading_rows[pl.ds(i, 1), :] * shift))
        feat = discount_rows[pl.ds(i, 1), :] * bond
        exact[i] = feat
        features[i] = feat.astype(BF16)
        return state

    early = dates - dates // 4
    state = lax.fori_loop(0, early, forward, start_state[...])
    part = flows.at[0, pl.ds(0, chips - 1)]
    pltpu.make_async_copy(part, part, recv_sems.at[0]).wait()
    share = pltpu.make_async_remote_copy(
        src_ref=flows.at[core],
        dst_ref=flows.at[core],
        send_sem=send_sems.at[1],
        recv_sem=recv_sems.at[1],
        device_id={"path": partner},
        device_id_type=MESH,
    )
    share.start()
    lax.fori_loop(early, dates, forward, state)
    pltpu.make_async_copy(part, part, send_sems.at[0]).wait()
    share.wait()

    rows = n * 2 * trades
    all_flows = flows[:, :, :, :half].reshape(rows, half)
    member = flows[:, :, :, half:].reshape(rows, sets)
    is_upper = (lax.broadcasted_iota(jnp.int32, (rows, sets), 0) // trades) % 2 == 1
    member_wide = member.astype(F32)
    member_low = jnp.where(is_upper, 0.0, member_wide).astype(BF16)
    member_high = jnp.where(is_upper, member_wide, 0.0).astype(BF16)
    net[:, :half] = dot(member_low, all_flows, TN).astype(BF16)
    net[:, half:] = dot(member_high, all_flows, TN)[:, : grid - half].astype(BF16)

    def value(i, carry):
        found = dot(features[i], net[...], NT)
        values[i] = found
        value_sums[me, pl.ds(i, 1), :] = jnp.sum(found, axis=0, keepdims=True)
        return carry

    lax.fori_loop(0, dates, value, 0)
    send_all(value_sums, 2)
    wait_all(value_sums, recv_sems, 2)
    offset = base_value[...] - jnp.sum(value_sums[...], axis=0) / paths_all
    weights = weight_rows[...]
    for i in range(dates):
        shifted = values[i] + offset[i : i + 1]
        slope = weights[i : i + 1] * jax.nn.sigmoid(SHARPNESS * shifted)
        values[i] = slope
        slope_sums[me, i : i + 1, :] = jnp.sum(slope, axis=0, keepdims=True)
    send_all(slope_sums, 3)
    weighted[...] = jnp.zeros_like(weighted)
    rate_acc[...] = jnp.zeros_like(rate_acc)
    wait_all(slope_sums, recv_sems, 3)
    loading_rows[...] = loading_rows[...] * jnp.exp(
        lax.broadcasted_iota(jnp.int32, (dates, grid), 0).astype(F32)
        * (-MEAN_REV * STEP_YEARS)
    )
    weight_rows[...] = jnp.sum(slope_sums[...], axis=0) / paths_all

    def backward(i, carry):
        adj = (values[i] - weight_rows[pl.ds(i, 1), :]).astype(BF16)
        adjoint[pl.ds(pl.multiple_of(i * paths, paths), paths), :] = adj
        product = dot(adj, net[...], NN) * exact[i]
        weighted[...] += loading_rows[pl.ds(i, 1), :] * product
        folded = jnp.sum(product.reshape(paths // 8, 8, grid), axis=0)
        rate_acc[...] += horizon_rows[pl.ds(i, 1), :] * folded
        return carry

    lax.fori_loop(0, dates, backward, 0)
    rate = jnp.sum(rate_acc[...], axis=0, keepdims=True) * (-1.0 / paths_all)
    lines = rate_sums.shape[1]
    for line in range(lines):
        first = 128 * line
        if first < grid:
            piece = rate[:, first : first + 128]
            rate_sums[me, line : line + 1, : piece.shape[1]] = piece
            if piece.shape[1] < 128:
                rate_sums[me, line : line + 1, piece.shape[1] :] = jnp.zeros(
                    (1, 128 - piece.shape[1]), F32
                )
        else:
            rate_sums[me, line : line + 1, :] = jnp.zeros((1, 128), F32)
    send_all(rate_sums, 4)

    sums = dot(adjoint[...], features[...].reshape(dates * paths, grid), TN) * (1.0 / paths_all)
    sums = jnp.concatenate([sums, jnp.zeros((sets, 2 * half - grid), F32)], axis=1)
    stacked = jnp.concatenate(split2(sums), axis=0)
    low_part = dot(all_flows, stacked[:, :half], NT)
    high_part = dot(all_flows, stacked[:, half:], NT)
    low_part = low_part[:, :sets] + low_part[:, sets:]
    high_part = high_part[:, :sets] + high_part[:, sets:]
    terms = jnp.where(is_upper, high_part, low_part) * member_wide
    terms = terms.reshape(2, chips, 2, trades, sets)
    alloc_sent[...] = terms[:, :, 0] + terms[:, :, 1]
    alloc_sums[me] = alloc_sent[core, chip]

    def send_alloc(step, carry):
        other = lax.rem(me + step, n)
        pltpu.make_async_remote_copy(
            src_ref=alloc_sent.at[other % 2, other // 2],
            dst_ref=alloc_sums.at[me],
            send_sem=send_sems.at[5],
            recv_sem=recv_sems.at[5],
            device_id={"path": other},
            device_id_type=MESH,
        ).start()
        return carry

    lax.fori_loop(1, n, send_alloc, 0)

    load_high, load_low = split2(factor_load[...])
    y_high, y_low = split2(weighted[...])
    local = dot(jnp.concatenate([load_high, load_low], axis=0), y_high, NT)
    local = local[:factors] + local[factors:] + dot(load_high, y_low, NT)
    start_out[...] = DECAY**dates * later_adjoint[...] - DECAY * local

    wait_all(rate_sums, recv_sems, 4)
    total = jnp.sum(rate_sums[...], axis=0)
    column = row_to_column(
        jnp.concatenate([total[line : line + 1] for line in range(lines)], axis=1)[:, :grid]
    )
    knot_out[...] = jnp.sum(spline[...] * column, axis=0, keepdims=True)

    wait_all(alloc_sums, recv_sems, 5)
    alloc_out[...] = column_to_row(
        jnp.sum(jnp.sum(alloc_sums[...], axis=0), axis=1, keepdims=True)
    )
    for buffer, which in ((value_sums, 2), (slope_sums, 3), (rate_sums, 4), (alloc_sums, 5)):
        wait_all(buffer, send_sems, which)


def per_device(
    normals,
    start_state,
    later_adjoint,
    vol,
    factor_load,
    knots,
    spline_jac,
    cashflows,
    trade_set,
    trade_end,
    set_cpty,
    default_prob,
    base_value,
):
    n = lax.axis_size("path")
    dates, factors, paths = normals.shape
    grid = knots.shape[0]
    trades = cashflows.shape[0]
    sets = base_value.shape[1]
    half = -(-grid // 256) * 128
    lines = -(-grid // 1024) * 8
    vmem = pl.BlockSpec(memory_space=pltpu.VMEM)
    smem = pl.BlockSpec(memory_space=pltpu.SMEM)
    knot_grad, alloc, start_adjoint = pl.pallas_call(
        functools.partial(kernel, n),
        out_shape=[
            jax.ShapeDtypeStruct((1, grid), F32),
            jax.ShapeDtypeStruct((1, trades), F32),
            jax.ShapeDtypeStruct((factors, paths), F32),
        ],
        in_specs=[smem, smem] + [vmem] * 5 + [pl.BlockSpec(memory_space=pl.ANY)] + [vmem] * 5,
        out_specs=[vmem] * 3,
        scratch_shapes=[
            pltpu.VMEM((grid, grid), F32),
            pltpu.VMEM((2, n // 2, 2 * trades, half + sets), BF16),
            pltpu.VMEM((n, dates, sets), F32),
            pltpu.VMEM((n, dates, sets), F32),
            pltpu.VMEM((n, lines, 128), F32),
            pltpu.VMEM((2, n // 2, trades, sets), F32),
            pltpu.VMEM((n, trades, sets), F32),
            pltpu.VMEM((sets, grid), BF16),
            pltpu.VMEM((dates, paths, grid), F32),
            pltpu.VMEM((dates, paths, grid), BF16),
            pltpu.VMEM((dates, paths, sets), F32),
            pltpu.VMEM((dates * paths, sets), BF16),
            pltpu.VMEM((paths, grid), F32),
            pltpu.VMEM((8, grid), F32),
            pltpu.VMEM((dates, grid), F32),
            pltpu.VMEM((dates, grid), F32),
            pltpu.VMEM((dates, grid), F32),
            pltpu.VMEM((dates, sets), F32),
            pltpu.VMEM((6 * factors, grid), BF16),
            pltpu.SemaphoreType.DMA,
            pltpu.SemaphoreType.DMA((6,)),
            pltpu.SemaphoreType.DMA((6,)),
        ],
        compiler_params=pltpu.CompilerParams(
            collective_id=0, has_side_effects=True, vmem_limit_bytes=56 * 1024 * 1024
        ),
    )(
        vol,
        trade_end,
        normals,
        start_state,
        later_adjoint,
        factor_load,
        knots.reshape(1, grid),
        spline_jac,
        cashflows,
        trade_set,
        set_cpty,
        default_prob,
        base_value,
    )
    return knot_grad.reshape(grid), alloc.reshape(trades), start_adjoint


def solution(mesh):
    in_specs = (
        P(None, None, ("group", "path")),
        P(None, ("group", "path")),
        P(None, ("group", "path")),
        P(),
        P(),
        P(),
        P(),
        P(("group", "path"), None),
        P(("group", "path"), None),
        P(("group", "path")),
        P("group", None),
        P(),
        P(None, "group"),
    )
    out_specs = (P("group"), P(("group", "path")), P(None, ("group", "path")))
    return jax.shard_map(
        per_device, mesh=mesh, in_specs=in_specs, out_specs=out_specs, check_vma=False
    )
```

time: 272 us -> 50.4 us (0.19)
  blocking collectives: 202 us -> 0 us
  Pallas kernels: 0 us -> 43.1 us
  matrix products: 42.6 us -> 0 us
  other arithmetic: 17.4 us -> 0 us
    psum x3 -> x0, blocking collectives: 118 us -> none  [the longest x1 41.2 us: per_device(): mean_slope = lax.psum(jnp.sum(slope, axis=2), 'path') / paths_all]
    all_gather x2 -> x0, blocking collectives: 83.6 us -> none  [the longest x1 42 us: per_device(): lax.all_gather(set_ids, 'path', axis=0, tiled=True)]
    pallas_call x0 -> x1, Pallas kernels: none -> 43.1 us  [per_device(): pl.pallas_call(functools.partial(kernel, n), out_shape=[jax.ShapeDtypeStr...]
    dot_general x9 -> x0, matrix products: 42.6 us -> none  [the longest x1 7.57 us: per_device(): jnp.einsum('fm,imp->ifp', factor_load, feat_adjoint * feat_exact * loadin...]
    unnamed x8 -> x0, other arithmetic: 12 us -> none
    unnamed x47 -> x5, local copies, waits for them, and re-layouts: 5.08 us -> 6.46 us
where the time goes in v1:
time: 50.4 us; the launch traced here: 50.2 us
  Pallas kernels  43.1 us (86%)
  local copies, waits for them, and re-layouts  6.46 us (13%)
  between operations  0.64 us (1%)
    pallas_call x1, Pallas kernels, per_device(): pl.pallas_call(functools.partial(kernel, n), out_shape=[jax.ShapeDtypeStr...  43.1 us
    unnamed x5, local copies, waits for them, and re-layouts  6.46 us

profile of v1, /device:TPU:0, one launch (start us, length us, event | category | flops | bytes accessed | tf_op | source)
XLA Modules:
  0.0 50.2 jit_solution(14060486698157285522)
XLA Ops:
  0.6 1.3 %copy.16.trade_set = s32[8,1]{1,0:T(8,128)} copy(s32[8,1]{0,1:T(1,128)} %param.21) | data formatting | bytes 64 | tf_op args[8]
  2.0 1.4 %copy.17.set_cpty = s32[128,1]{1,0:T(8,128)} copy(s32[128,1]{0,1:T(1,128)} %param.23) | data formatting | bytes 1024 | tf_op args[10]
  3.3 43.1 %shard_map.148 = (f32[1,960]{1,0:T(1,128)}, f32[1,8]{1,0:T(1,128)}, f32[32,256]{1,0:T(8,128)}) custom-call(f32[8]{0:T(128)} %vol.1, s32[8]{0:T(128)} %trade_end.1, f32[8,32,256]{2,1,0:T(8,128)} %normals.1, f32[32,256]{1,0:T(8,128)} %start_state.1, f32[32,256]{1,0:T(8,128)} %later_adjoint.1, f32[32,960]{1,0:T(8,128)} %factor_load.1, f32[1,960]{1,0:T(1,128)} %bitcast.3, ...), custom_call_target="tpu_custom_call" | custom-call | tf_op jit(solution)/shard_map/pallas_call | solution.py:374
  46.4 1.3 %copy.21 = f32[960]{0:T(1024)} copy(f32[960]{0:T(1024)} %bitcast.4) | data formatting | bytes 7680
  47.7 1.1 %copy.22 = f32[8]{0:T(128)} copy(f32[8]{0:T(128)} %bitcast.5) | data formatting | bytes 64
  48.8 1.4 %copy.23 = f32[32,256]{1,0:T(8,128)} copy(f32[32,256]{1,0:T(8,128)} %get-tuple-element.14) | data formatting | bytes 65536

commit v2 on v1

--- a/solution.py
+++ b/solution.py
@@ -72,15 +72,14 @@
 def kernel(
     n,
     vol,
+    trade_set,
     trade_end,
     normals,
     start_state,
-    later_adjoint,
     factor_load,
     knots,
     spline_hbm,
     cashflows,
-    trade_set,
     set_cpty,
     default_prob,
     base_value,
@@ -89,10 +88,15 @@
     start_out,
     spline,
     flows,
+    value_pair,
     value_sums,
+    slope_pair,
     slope_sums,
+    rate_pair,
     rate_sums,
     alloc_sent,
+    alloc_pair,
+    alloc_chip,
     alloc_sums,
     net,
     exact,
@@ -128,16 +132,19 @@
 
     def greet(step, carry):
         pl.semaphore_signal(
-            barrier, inc=1, device_id={"path": lax.rem(me + step, n)}, device_id_type=MESH
+            barrier, inc=1, device_id={"path": lax.rem(me + 2 * step, n)}, device_id_type=MESH
         )
         return carry
 
-    lax.fori_loop(1, n, greet, 0)
+    lax.fori_loop(1, chips, greet, 0)
+    pl.semaphore_signal(barrier, inc=1, device_id={"path": partner}, device_id_type=MESH)
 
     end = jnp.zeros((trades, 1), jnp.int32)
+    set_id = jnp.zeros((trades, 1), jnp.int32)
     for trade in range(trades):
         at = lax.broadcasted_iota(jnp.int32, (trades, 1), 0) == trade
         end = jnp.where(at, trade_end[trade], end)
+        set_id = jnp.where(at, trade_set[trade], set_id)
     live = jnp.where(
         lax.broadcasted_iota(jnp.int32, (trades, grid), 1) < end,
         cashflows[...].astype(F32),
@@ -146,7 +153,7 @@
     upper = jnp.concatenate(
         [live[:, half:], jnp.zeros((trades, 2 * half - grid), F32)], axis=1
     )
-    one_hot = (lax.broadcasted_iota(jnp.int32, (trades, sets), 1) == trade_set[...]).astype(F32)
+    one_hot = (lax.broadcasted_iota(jnp.int32, (trades, sets), 1) == set_id).astype(F32)
     message = jnp.concatenate(
         [
             jnp.concatenate([live[:, :half], upper], axis=0),
@@ -156,7 +163,7 @@
     )
     flows[core, chip] = message.astype(BF16)
 
-    pl.semaphore_wait(barrier, n - 1)
+    pl.semaphore_wait(barrier, chips)
 
     def send_flows(step, carry):
         pltpu.make_async_remote_copy(
@@ -171,23 +178,40 @@
 
     lax.fori_loop(1, chips, send_flows, 0)
 
-    def send_all(buffer, which):
+    def send_pair(buffer, target, which):
+        copy = pltpu.make_async_remote_copy(
+            src_ref=buffer,
+            dst_ref=target,
+            send_sem=send_sems.at[which],
+            recv_sem=recv_sems.at[which],
+            device_id={"path": partner},
+            device_id_type=MESH,
+        )
+        copy.start()
+        return copy
+
+    def send_chips(source, buffer, which):
         def send(step, carry):
+            other = lax.rem(chip + step, chips)
             pltpu.make_async_remote_copy(
-                src_ref=buffer.at[me],
-                dst_ref=buffer.at[me],
+                src_ref=source(other),
+                dst_ref=buffer.at[chip],
                 send_sem=send_sems.at[which],
                 recv_sem=recv_sems.at[which],
-                device_id={"path": lax.rem(me + step, n)},
+                device_id={"path": 2 * other + core},
                 device_id_type=MESH,
             ).start()
             return carry
 
-        lax.fori_loop(1, n, send, 0)
-
-    def wait_all(buffer, sems, which):
-        others = buffer.at[pl.ds(0, n - 1)]
+        lax.fori_loop(1, chips, send, 0)
+
+    def wait_chips(buffer, sems, which):
+        others = buffer.at[pl.ds(0, chips - 1)]
         pltpu.make_async_copy(others, others, sems.at[which]).wait()
+
+    def send_sum(pair, sums, which):
+        sums[chip] = pair[0] + pair[1]
+        send_chips(lambda other: sums.at[chip], sums, which)
 
     index = lax.broadcasted_iota(jnp.int32, (dates, grid), 1)
     date = lax.broadcasted_iota(jnp.int32, (dates, grid), 0)
@@ -202,10 +226,10 @@
     discount_rows[...] = jnp.where(alive, jnp.exp(-zero_rate * horizon), 0.0)
 
     counter = (
-        lax.broadcasted_iota(jnp.int32, (sets, default_prob.shape[1]), 1) == set_cpty[...]
+        lax.broadcasted_iota(jnp.int32, (default_prob.shape[1], sets), 0) == set_cpty[...]
     ).astype(F32)
     weight_rows[...] = LOSS_RATE * dot(
-        default_prob[...], counter, NT, precision=lax.Precision.HIGHEST
+        default_prob[...], counter, NN, precision=lax.Precision.HIGHEST
     )
 
     high, mid, low = split3(factor_load[...])
@@ -252,23 +276,25 @@
     def value(i, carry):
         found = dot(features[i], net[...], NT)
         values[i] = found
-        value_sums[me, pl.ds(i, 1), :] = jnp.sum(found, axis=0, keepdims=True)
+        value_pair[core, pl.ds(i, 1), :] = jnp.sum(found, axis=0, keepdims=True)
         return carry
 
     lax.fori_loop(0, dates, value, 0)
-    send_all(value_sums, 2)
-    wait_all(value_sums, recv_sems, 2)
+    send_pair(value_pair.at[core], value_pair.at[core], 2).wait()
+    send_sum(value_pair, value_sums, 3)
+    wait_chips(value_sums, recv_sems, 3)
     offset = base_value[...] - jnp.sum(value_sums[...], axis=0) / paths_all
     weights = weight_rows[...]
     for i in range(dates):
         shifted = values[i] + offset[i : i + 1]
         slope = weights[i : i + 1] * jax.nn.sigmoid(SHARPNESS * shifted)
         values[i] = slope
-        slope_sums[me, i : i + 1, :] = jnp.sum(slope, axis=0, keepdims=True)
-    send_all(slope_sums, 3)
+        slope_pair[core, i : i + 1, :] = jnp.sum(slope, axis=0, keepdims=True)
+    send_pair(slope_pair.at[core], slope_pair.at[core], 4).wait()
+    send_sum(slope_pair, slope_sums, 5)
     weighted[...] = jnp.zeros_like(weighted)
     rate_acc[...] = jnp.zeros_like(rate_acc)
-    wait_all(slope_sums, recv_sems, 3)
+    wait_chips(slope_sums, recv_sems, 5)
     loading_rows[...] = loading_rows[...] * jnp.exp(
         lax.broadcasted_iota(jnp.int32, (dates, grid), 0).astype(F32)
         * (-MEAN_REV * STEP_YEARS)
@@ -291,14 +317,14 @@
         first = 128 * line
         if first < grid:
             piece = rate[:, first : first + 128]
-            rate_sums[me, line : line + 1, : piece.shape[1]] = piece
+            rate_pair[core, line : line + 1, : piece.shape[1]] = piece
             if piece.shape[1] < 128:
-                rate_sums[me, line : line + 1, piece.shape[1] :] = jnp.zeros(
+                rate_pair[core, line : line + 1, piece.shape[1] :] = jnp.zeros(
                     (1, 128 - piece.shape[1]), F32
                 )
         else:
-            rate_sums[me, line : line + 1, :] = jnp.zeros((1, 128), F32)
-    send_all(rate_sums, 4)
+            rate_pair[core, line : line + 1, :] = jnp.zeros((1, 128), F32)
+    rate_copy = send_pair(rate_pair.at[core], rate_pair.at[core], 6)
 
     sums = dot(adjoint[...], features[...].reshape(dates * paths, grid), TN) * (1.0 / paths_all)
     sums = jnp.concatenate([sums, jnp.zeros((sets, 2 * half - grid), F32)], axis=1)
@@ -310,41 +336,39 @@
     terms = jnp.where(is_upper, high_part, low_part) * member_wide
     terms = terms.reshape(2, chips, 2, trades, sets)
     alloc_sent[...] = terms[:, :, 0] + terms[:, :, 1]
-    alloc_sums[me] = alloc_sent[core, chip]
-
-    def send_alloc(step, carry):
-        other = lax.rem(me + step, n)
-        pltpu.make_async_remote_copy(
-            src_ref=alloc_sent.at[other % 2, other // 2],
-            dst_ref=alloc_sums.at[me],
-            send_sem=send_sems.at[5],
-            recv_sem=recv_sems.at[5],
-            device_id={"path": other},
-            device_id_type=MESH,
-        ).start()
-        return carry
-
-    lax.fori_loop(1, n, send_alloc, 0)
+    alloc_copy = send_pair(alloc_sent.at[1 - core], alloc_pair, 8)
+    rate_copy.wait()
+    send_sum(rate_pair, rate_sums, 7)
 
     load_high, load_low = split2(factor_load[...])
     y_high, y_low = split2(weighted[...])
     local = dot(jnp.concatenate([load_high, load_low], axis=0), y_high, NT)
     local = local[:factors] + local[factors:] + dot(load_high, y_low, NT)
-    start_out[...] = DECAY**dates * later_adjoint[...] - DECAY * local
-
-    wait_all(rate_sums, recv_sems, 4)
+    start_out[...] = local
+    alloc_copy.wait()
+    alloc_chip[...] = alloc_sent[core] + alloc_pair[...]
+    alloc_sums[chip] = alloc_chip[chip]
+    send_chips(lambda other: alloc_chip.at[other], alloc_sums, 9)
+
+    wait_chips(rate_sums, recv_sems, 7)
     total = jnp.sum(rate_sums[...], axis=0)
     column = row_to_column(
         jnp.concatenate([total[line : line + 1] for line in range(lines)], axis=1)[:, :grid]
     )
     knot_out[...] = jnp.sum(spline[...] * column, axis=0, keepdims=True)
 
-    wait_all(alloc_sums, recv_sems, 5)
+    wait_chips(alloc_sums, recv_sems, 9)
     alloc_out[...] = column_to_row(
         jnp.sum(jnp.sum(alloc_sums[...], axis=0), axis=1, keepdims=True)
     )
-    for buffer, which in ((value_sums, 2), (slope_sums, 3), (rate_sums, 4), (alloc_sums, 5)):
-        wait_all(buffer, send_sems, which)
+    for buffer, which in ((value_sums, 3), (slope_sums, 5), (rate_sums, 7), (alloc_sums, 9)):
+        wait_chips(buffer, send_sems, which)
+
+
+def finish(knot_part, alloc_part, local, later_adjoint, knot_out, alloc_out, start_out, *, dates):
+    knot_out[...] = knot_part[...]
+    alloc_out[...] = alloc_part[...]
+    start_out[...] = DECAY**dates * later_adjoint[...] - DECAY * local[...]
 
 
 def per_device(
@@ -371,23 +395,29 @@
     lines = -(-grid // 1024) * 8
     vmem = pl.BlockSpec(memory_space=pltpu.VMEM)
     smem = pl.BlockSpec(memory_space=pltpu.SMEM)
-    knot_grad, alloc, start_adjoint = pl.pallas_call(
+    out_shape = [
+        jax.ShapeDtypeStruct((1, grid), F32),
+        jax.ShapeDtypeStruct((1, trades), F32),
+        jax.ShapeDtypeStruct((factors, paths), F32),
+    ]
+    parts = pl.pallas_call(
         functools.partial(kernel, n),
-        out_shape=[
-            jax.ShapeDtypeStruct((1, grid), F32),
-            jax.ShapeDtypeStruct((1, trades), F32),
-            jax.ShapeDtypeStruct((factors, paths), F32),
-        ],
-        in_specs=[smem, smem] + [vmem] * 5 + [pl.BlockSpec(memory_space=pl.ANY)] + [vmem] * 5,
+        out_shape=out_shape,
+        in_specs=[smem] * 3 + [vmem] * 4 + [pl.BlockSpec(memory_space=pltpu.HBM)] + [vmem] * 4,
         out_specs=[vmem] * 3,
         scratch_shapes=[
             pltpu.VMEM((grid, grid), F32),
             pltpu.VMEM((2, n // 2, 2 * trades, half + sets), BF16),
-            pltpu.VMEM((n, dates, sets), F32),
-            pltpu.VMEM((n, dates, sets), F32),
-            pltpu.VMEM((n, lines, 128), F32),
+            pltpu.VMEM((2, dates, sets), F32),
+            pltpu.VMEM((n // 2, dates, sets), F32),
+            pltpu.VMEM((2, dates, sets), F32),
+            pltpu.VMEM((n // 2, dates, sets), F32),
+            pltpu.VMEM((2, lines, 128), F32),
+            pltpu.VMEM((n // 2, lines, 128), F32),
             pltpu.VMEM((2, n // 2, trades, sets), F32),
-            pltpu.VMEM((n, trades, sets), F32),
+            pltpu.VMEM((n // 2, trades, sets), F32),
+            pltpu.VMEM((n // 2, trades, sets), F32),
+            pltpu.VMEM((n // 2, trades, sets), F32),
             pltpu.VMEM((sets, grid), BF16),
             pltpu.VMEM((dates, paths, grid), F32),
             pltpu.VMEM((dates, paths, grid), BF16),
@@ -401,27 +431,32 @@
             pltpu.VMEM((dates, sets), F32),
             pltpu.VMEM((6 * factors, grid), BF16),
             pltpu.SemaphoreType.DMA,
-            pltpu.SemaphoreType.DMA((6,)),
-            pltpu.SemaphoreType.DMA((6,)),
+            pltpu.SemaphoreType.DMA((10,)),
+            pltpu.SemaphoreType.DMA((10,)),
         ],
         compiler_params=pltpu.CompilerParams(
-            collective_id=0, has_side_effects=True, vmem_limit_bytes=56 * 1024 * 1024
+            collective_id=0, has_side_effects=True, vmem_limit_bytes=50 * 1024 * 1024
         ),
     )(
         vol,
+        trade_set.reshape(trades),
         trade_end,
         normals,
         start_state,
-        later_adjoint,
         factor_load,
         knots.reshape(1, grid),
         spline_jac,
         cashflows,
-        trade_set,
-        set_cpty,
+        set_cpty.reshape(1, sets),
         default_prob,
         base_value,
     )
+    knot_grad, alloc, start_adjoint = pl.pallas_call(
+        functools.partial(finish, dates=dates),
+        out_shape=out_shape,
+        in_specs=[vmem] * 4,
+        out_specs=[vmem] * 3,
+    )(*parts, later_adjoint)
     return knot_grad.reshape(grid), alloc.reshape(trades), start_adjoint
 
 

time: 50.4 us -> 54.4 us (1.079)
  local copies, waits for them, and re-layouts: 6.46 us -> 9.77 us
    unnamed x5 -> x28, local copies, waits for them, and re-layouts: 6.46 us -> 9.77 us
    pallas_call x1 -> x2, Pallas kernels: 43.1 us -> 43.5 us  [the longest x1 42.1 us: per_device(): pl.pallas_call(functools.partial(kernel, n), out_shape=out_shape, in_spec...]
where the time goes in v2:
time: 54.4 us; the launch traced here: 53.9 us
  Pallas kernels  43.5 us (80%)
  local copies, waits for them, and re-layouts  9.77 us (18%)
  between operations  0.67 us (1%)
    pallas_call x1, Pallas kernels, per_device(): pl.pallas_call(functools.partial(kernel, n), out_shape=out_shape, in_spec...  42.1 us
    unnamed x28, local copies, waits for them, and re-layouts  9.77 us
    pallas_call x1, Pallas kernels, per_device(): pl.pallas_call(functools.partial(finish, dates=dates), out_shape=out_shap...  1.41 us

profile of v2, /device:TPU:0, one launch (start us, length us, event | category | flops | bytes accessed | tf_op | source)
XLA Modules:
  0.0 53.9 jit_solution(8841538916743999040)
XLA Ops:
  0.6 0.0 copy-start
  0.6 0.9 %copy-done = f32[8,32,256]{2,1,0:T(8,128)S(1)} copy-done((f32[8,32,256]{2,1,0:T(8,128)S(1)}, f32[8,32,256]{2,1,0:T(8,128)}, u32[]{:S(2)}) %copy-start) | copy-done | bytes 262168
  1.6 0.0 copy-start.1
  1.6 0.9 %copy-done.1 = f32[32,960]{1,0:T(8,128)S(1)} copy-done((f32[32,960]{1,0:T(8,128)S(1)}, f32[32,960]{1,0:T(8,128)}, u32[]{:S(2)}) %copy-start.1) | copy-done | bytes 122904
  2.5 0.0 copy-start.2
  2.5 0.8 %copy-done.2 = f32[32,256]{1,0:T(8,128)S(1)} copy-done((f32[32,256]{1,0:T(8,128)S(1)}, f32[32,256]{1,0:T(8,128)}, u32[]{:S(2)}) %copy-start.2) | copy-done | bytes 32792
  3.2 0.0 copy-start.4
  3.3 0.7 %copy-done.4 = bf16[8,960]{1,0:T(8,128)(2,1)S(1)} copy-done((bf16[8,960]{1,0:T(8,128)(2,1)S(1)}, bf16[8,960]{1,0:T(8,128)(2,1)}, u32[]{:S(2)}) %copy-start.4) | copy-done | bytes 15384
  4.0 0.0 copy-start.5
  4.0 0.7 %copy-done.5 = f32[960]{0:T(1024)S(1)} copy-done((f32[960]{0:T(1024)S(1)}, f32[960]{0:T(1024)}, u32[]{:S(2)}) %copy-start.5) | copy-done | bytes 3864
  4.7 0.0 copy-start.6
  4.7 0.7 %copy-done.6 = f32[8,64]{1,0:T(8,128)S(1)} copy-done((f32[8,64]{1,0:T(8,128)S(1)}, f32[8,64]{1,0:T(8,128)}, u32[]{:S(2)}) %copy-start.6) | copy-done | bytes 2072
  5.3 0.0 copy-start.7
  5.3 0.7 %copy-done.7 = f32[8,128]{1,0:T(8,128)S(1)} copy-done((f32[8,128]{1,0:T(8,128)S(1)}, f32[8,128]{1,0:T(8,128)}, u32[]{:S(2)}) %copy-start.7) | copy-done | bytes 4120
  6.0 0.0 copy-start.9
  6.0 0.7 %copy-done.9 = f32[8]{0:T(128)S(1)} copy-done((f32[8]{0:T(128)S(1)}, f32[8]{0:T(128)}, u32[]{:S(2)}) %copy-start.9) | copy-done | bytes 56
  6.7 0.0 copy-start.10
  6.7 0.7 %copy-done.10 = s32[8,1]{0,1:T(1,128)S(1)} copy-done((s32[8,1]{0,1:T(1,128)S(1)}, s32[8,1]{0,1:T(1,128)}, u32[]{:S(2)}) %copy-start.10) | copy-done | bytes 56
  7.3 0.0 copy-start.11
  7.3 0.7 %copy-done.11 = s32[8]{0:T(128)S(1)} copy-done((s32[8]{0:T(128)S(1)}, s32[8]{0:T(128)}, u32[]{:S(2)}) %copy-start.11) | copy-done | bytes 56
  8.0 0.0 copy-start.12
  8.0 0.7 %copy-done.12 = s32[128,1]{0,1:T(1,128)S(1)} copy-done((s32[128,1]{0,1:T(1,128)S(1)}, s32[128,1]{0,1:T(1,128)}, u32[]{:S(2)}) %copy-start.12) | copy-done | bytes 536
  8.7 42.1 %shard_map.148 = (f32[1,960]{1,0:T(1,128)S(1)}, f32[1,8]{1,0:T(1,128)S(1)}, f32[32,256]{1,0:T(8,128)S(1)}) custom-call(f32[8]{0:T(128)S(1)} %copy-done.9, s32[8]{0:T(128)S(1)} %bitcast.6, s32[8]{0:T(128)S(1)} %copy-done.11, f32[8,32,256]{2,1,0:T(8,128)S(1)} %copy-done, f32[32,256]{1,0:T(8,128)S(1)} %copy-done.2, f32[32,960]{1,0:T(8,128)S(1)} %copy-done.1, ...), custom_call_target="tpu_custom_call" | custom-call | tf_op jit(solution)/shard_map/pallas_call | solution.py:403
  50.7 0.0 copy-start.3
  50.7 0.6 %copy-done.3 = f32[32,256]{1,0:T(8,128)} copy-done((f32[32,256]{1,0:T(8,128)}, f32[32,256]{1,0:T(8,128)S(1)}, u32[]{:S(2)}) %copy-start.3) | copy-done | bytes 32792
  51.3 0.0 copy-start.8
  51.3 0.6 %copy-done.8 = f32[1,960]{1,0:T(1,128)} copy-done((f32[1,960]{1,0:T(1,128)}, f32[1,960]{1,0:T(1,128)S(1)}, u32[]{:S(2)}) %copy-start.8) | copy-done | bytes 3864
  51.9 0.0 copy-start.13
  51.9 0.6 %copy-done.13 = f32[1,8]{1,0:T(1,128)} copy-done((f32[1,8]{1,0:T(1,128)}, f32[1,8]{1,0:T(1,128)S(1)}, u32[]{:S(2)}) %copy-start.13) | copy-done | bytes 56
  52.5 1.4 %shard_map.149 = (f32[1,960]{1,0:T(1,128)}, f32[1,8]{1,0:T(1,128)}, f32[32,256]{1,0:T(8,128)}) custom-call(f32[1,960]{1,0:T(1,128)} %copy-done.8, f32[1,8]{1,0:T(1,128)} %copy-done.13, f32[32,256]{1,0:T(8,128)} %copy-done.3, f32[32,256]{1,0:T(8,128)} %later_adjoint.1), custom_call_target="tpu_custom_call" | custom-call | tf_op jit(solution)/shard_map/pallas_call | solution.py:454
Async XLA Ops:
  0.6 1.0 %copy-start = (f32[8,32,256]{2,1,0:T(8,128)S(1)}, f32[8,32,256]{2,1,0:T(8,128)}, u32[]{:S(2)}) copy-start(f32[8,32,256]{2,1,0:T(8,128)} %normals.1) | copy-start | bytes 786436
  1.6 0.9 %copy-start.1 = (f32[32,960]{1,0:T(8,128)S(1)}, f32[32,960]{1,0:T(8,128)}, u32[]{:S(2)}) copy-start(f32[32,960]{1,0:T(8,128)} %factor_load.1) | copy-start | bytes 368644
  2.5 0.8 %copy-start.2 = (f32[32,256]{1,0:T(8,128)S(1)}, f32[32,256]{1,0:T(8,128)}, u32[]{:S(2)}) copy-start(f32[32,256]{1,0:T(8,128)} %start_state.1) | copy-start | bytes 98308
  3.2 0.7 %copy-start.4 = (bf16[8,960]{1,0:T(8,128)(2,1)S(1)}, bf16[8,960]{1,0:T(8,128)(2,1)}, u32[]{:S(2)}) copy-start(bf16[8,960]{1,0:T(8,128)(2,1)} %cashflows.1) | copy-start | bytes 46084
  4.0 0.7 %copy-start.5 = (f32[960]{0:T(1024)S(1)}, f32[960]{0:T(1024)}, u32[]{:S(2)}) copy-start(f32[960]{0:T(1024)} %param.18) | copy-start | bytes 11524
  4.7 0.7 %copy-start.6 = (f32[8,64]{1,0:T(8,128)S(1)}, f32[8,64]{1,0:T(8,128)}, u32[]{:S(2)}) copy-start(f32[8,64]{1,0:T(8,128)} %default_prob.1) | copy-start | bytes 6148
  5.3 0.7 %copy-start.7 = (f32[8,128]{1,0:T(8,128)S(1)}, f32[8,128]{1,0:T(8,128)}, u32[]{:S(2)}) copy-start(f32[8,128]{1,0:T(8,128)} %base_value.1) | copy-start | bytes 12292
  6.0 0.7 %copy-start.9 = (f32[8]{0:T(128)S(1)}, f32[8]{0:T(128)}, u32[]{:S(2)}) copy-start(f32[8]{0:T(128)} %vol.1) | copy-start | bytes 100
  6.7 0.7 %copy-start.10 = (s32[8,1]{0,1:T(1,128)S(1)}, s32[8,1]{0,1:T(1,128)}, u32[]{:S(2)}) copy-start(s32[8,1]{0,1:T(1,128)} %param.21) | copy-start | bytes 100
  7.3 0.7 %copy-start.11 = (s32[8]{0:T(128)S(1)}, s32[8]{0:T(128)}, u32[]{:S(2)}) copy-start(s32[8]{0:T(128)} %trade_end.1) | copy-start | bytes 100
  8.0 0.7 %copy-start.12 = (s32[128,1]{0,1:T(1,128)S(1)}, s32[128,1]{0,1:T(1,128)}, u32[]{:S(2)}) copy-start(s32[128,1]{0,1:T(1,128)} %param.23) | copy-start | bytes 1540
  50.7 0.6 %copy-start.3 = (f32[32,256]{1,0:T(8,128)}, f32[32,256]{1,0:T(8,128)S(1)}, u32[]{:S(2)}) copy-start(f32[32,256]{1,0:T(8,128)S(1)} %get-tuple-element.11.local) | copy-start | bytes 98308
  51.3 0.6 %copy-start.8 = (f32[1,960]{1,0:T(1,128)}, f32[1,960]{1,0:T(1,128)S(1)}, u32[]{:S(2)}) copy-start(f32[1,960]{1,0:T(1,128)S(1)} %get-tuple-element.9.knot_part) | copy-start | bytes 11524
  51.9 0.6 %copy-start.13 = (f32[1,8]{1,0:T(1,128)}, f32[1,8]{1,0:T(1,128)S(1)}, u32[]{:S(2)}) copy-start(f32[1,8]{1,0:T(1,128)S(1)} %get-tuple-element.10.alloc_part) | copy-start | bytes 100

commit v3 on v2

--- a/solution.py
+++ b/solution.py
@@ -71,22 +71,37 @@
 
 def kernel(
     n,
-    vol,
+    cashflows,
+    trade_set_hbm,
+    trade_end_hbm,
+    spline_hbm,
+    knots_hbm,
+    factor_load_hbm,
+    vol_hbm,
+    start_state_hbm,
+    normals_hbm,
+    set_cpty_hbm,
+    default_prob_hbm,
+    base_value_hbm,
+    later_adjoint_hbm,
+    knot_hbm,
+    alloc_hbm,
+    start_hbm,
     trade_set,
     trade_end,
+    spline,
+    knots,
+    factor_load,
+    vol,
+    start_state,
     normals,
-    start_state,
-    factor_load,
-    knots,
-    spline_hbm,
-    cashflows,
     set_cpty,
     default_prob,
     base_value,
+    later_adjoint,
     knot_out,
     alloc_out,
     start_out,
-    spline,
     flows,
     value_pair,
     value_sums,
@@ -110,7 +125,9 @@
     horizon_rows,
     weight_rows,
     load_split,
-    spline_sem,
+    exact_sums,
+    load_sems,
+    store_sems,
     send_sems,
     recv_sems,
 ):
@@ -125,8 +142,23 @@
     chip, core = me // 2, me % 2
     partner = me + 1 - 2 * core
 
-    spline_copy = pltpu.make_async_copy(spline_hbm, spline, spline_sem)
-    spline_copy.start()
+    loads = []
+    for source, target in (
+        (trade_set_hbm, trade_set),
+        (trade_end_hbm, trade_end),
+        (spline_hbm, spline),
+        (knots_hbm, knots),
+        (factor_load_hbm, factor_load),
+        (vol_hbm, vol),
+        (start_state_hbm, start_state),
+        (normals_hbm, normals),
+        (set_cpty_hbm, set_cpty),
+        (default_prob_hbm, default_prob),
+        (base_value_hbm, base_value),
+        (later_adjoint_hbm, later_adjoint),
+    ):
+        loads.append(pltpu.make_async_copy(source, target, load_sems.at[len(loads)]))
+        loads[-1].start()
 
     barrier = pltpu.get_barrier_semaphore()
 
@@ -139,12 +171,10 @@
     lax.fori_loop(1, chips, greet, 0)
     pl.semaphore_signal(barrier, inc=1, device_id={"path": partner}, device_id_type=MESH)
 
-    end = jnp.zeros((trades, 1), jnp.int32)
-    set_id = jnp.zeros((trades, 1), jnp.int32)
-    for trade in range(trades):
-        at = lax.broadcasted_iota(jnp.int32, (trades, 1), 0) == trade
-        end = jnp.where(at, trade_end[trade], end)
-        set_id = jnp.where(at, trade_set[trade], set_id)
+    loads[0].wait()
+    loads[1].wait()
+    set_id = row_to_column(trade_set[...].astype(F32)).astype(jnp.int32)
+    end = row_to_column(trade_end[...].astype(F32)).astype(jnp.int32)
     live = jnp.where(
         lax.broadcasted_iota(jnp.int32, (trades, grid), 1) < end,
         cashflows[...].astype(F32),
@@ -221,7 +251,8 @@
     horizon = jnp.where(alive, maturity - fixing, 0.0)
     horizon_rows[...] = horizon
     loading_rows[...] = (1.0 - jnp.exp(-MEAN_REV * horizon)) / MEAN_REV
-    spline_copy.wait()
+    for load in loads[2:]:
+        load.wait()
     zero_rate = column_to_row(jnp.sum(spline[...] * knots[...], axis=1, keepdims=True))
     discount_rows[...] = jnp.where(alive, jnp.exp(-zero_rate * horizon), 0.0)
 
@@ -236,7 +267,9 @@
     load_split[...] = jnp.concatenate([high, high, mid, high, mid, low], axis=0)
 
     def forward(i, state):
-        state = DECAY * state + vol[i] * normals[i]
+        here = lax.broadcasted_iota(jnp.int32, (1, dates), 1) == i
+        date_vol = jnp.sum(jnp.where(here, vol[...], 0.0), axis=1, keepdims=True)
+        state = DECAY * state + date_vol * normals[i]
         s_high, s_mid, s_low = split3(state)
         stacked = jnp.concatenate([s_high, s_mid, s_high, s_low, s_mid, s_high], axis=0)
         shift = dot(stacked, load_split[...], TN)
@@ -244,6 +277,7 @@
         feat = discount_rows[pl.ds(i, 1), :] * bond
         exact[i] = feat
         features[i] = feat.astype(BF16)
+        exact_sums[pl.ds(i, 1), :] = jnp.sum(feat, axis=0, keepdims=True)
         return state
 
     early = dates - dates // 4
@@ -288,30 +322,43 @@
     for i in range(dates):
         shifted = values[i] + offset[i : i + 1]
         slope = weights[i : i + 1] * jax.nn.sigmoid(SHARPNESS * shifted)
-        values[i] = slope
-        slope_pair[core, i : i + 1, :] = jnp.sum(slope, axis=0, keepdims=True)
-    send_pair(slope_pair.at[core], slope_pair.at[core], 4).wait()
-    send_sum(slope_pair, slope_sums, 5)
+        total = jnp.sum(slope, axis=0, keepdims=True)
+        slope_pair[core, i : i + 1, :] = total
+        adjoint[i * paths : (i + 1) * paths, :sets] = (slope - total / paths).astype(BF16)
+    slope_copy = send_pair(slope_pair.at[core], slope_pair.at[core], 4)
+    adjoint[:, sets:] = (
+        lax.broadcasted_iota(jnp.int32, (dates * paths, 128), 0) // paths
+        == lax.broadcasted_iota(jnp.int32, (dates * paths, 128), 1)
+    ).astype(BF16)
     weighted[...] = jnp.zeros_like(weighted)
     rate_acc[...] = jnp.zeros_like(rate_acc)
-    wait_chips(slope_sums, recv_sems, 5)
     loading_rows[...] = loading_rows[...] * jnp.exp(
         lax.broadcasted_iota(jnp.int32, (dates, grid), 0).astype(F32)
         * (-MEAN_REV * STEP_YEARS)
     )
-    weight_rows[...] = jnp.sum(slope_sums[...], axis=0) / paths_all
 
     def backward(i, carry):
-        adj = (values[i] - weight_rows[pl.ds(i, 1), :]).astype(BF16)
-        adjoint[pl.ds(pl.multiple_of(i * paths, paths), paths), :] = adj
+        adj = adjoint[pl.ds(pl.multiple_of(i * paths, paths), paths), :sets]
         product = dot(adj, net[...], NN) * exact[i]
         weighted[...] += loading_rows[pl.ds(i, 1), :] * product
         folded = jnp.sum(product.reshape(paths // 8, 8, grid), axis=0)
         rate_acc[...] += horizon_rows[pl.ds(i, 1), :] * folded
         return carry
 
-    lax.fori_loop(0, dates, backward, 0)
-    rate = jnp.sum(rate_acc[...], axis=0, keepdims=True) * (-1.0 / paths_all)
+    lax.fori_loop(0, dates // 4, backward, 0)
+    slope_copy.wait()
+    send_sum(slope_pair, slope_sums, 5)
+    lax.fori_loop(dates // 4, dates, backward, 0)
+    sums = dot(adjoint[...], features[...].reshape(dates * paths, grid), TN)
+
+    wait_chips(slope_sums, recv_sems, 5)
+    remainder = slope_pair[core] / paths - jnp.sum(slope_sums[...], axis=0) / paths_all
+    common = dot(jnp.concatenate(split2(remainder), axis=0), net[...], NN)
+    common = common[:dates] + common[dates:]
+    rate = jnp.sum(rate_acc[...], axis=0, keepdims=True) + jnp.sum(
+        horizon_rows[...] * common * exact_sums[...], axis=0, keepdims=True
+    )
+    rate = rate * (-1.0 / paths_all)
     lines = rate_sums.shape[1]
     for line in range(lines):
         first = 128 * line
@@ -326,7 +373,10 @@
             rate_pair[core, line : line + 1, :] = jnp.zeros((1, 128), F32)
     rate_copy = send_pair(rate_pair.at[core], rate_pair.at[core], 6)
 
-    sums = dot(adjoint[...], features[...].reshape(dates * paths, grid), TN) * (1.0 / paths_all)
+    sums = sums[:sets] + dot(
+        remainder, sums[sets : sets + dates], TN, precision=lax.Precision.HIGHEST
+    )
+    sums = sums * (1.0 / paths_all)
     sums = jnp.concatenate([sums, jnp.zeros((sets, 2 * half - grid), F32)], axis=1)
     stacked = jnp.concatenate(split2(sums), axis=0)
     low_part = dot(all_flows, stacked[:, :half], NT)
@@ -340,15 +390,30 @@
     rate_copy.wait()
     send_sum(rate_pair, rate_sums, 7)
 
+    loading_rows[...] = loading_rows[...] * common
+    block = 32
+
+    def add_common(step, carry):
+        at = pl.ds(pl.multiple_of(step * block, block), block)
+        held = weighted[at, :]
+        for i in range(dates):
+            held = held + loading_rows[i : i + 1, :] * exact[i, at, :]
+        weighted[at, :] = held
+        return carry
+
+    lax.fori_loop(0, paths // block, add_common, 0)
+    alloc_copy.wait()
+    alloc_chip[...] = alloc_sent[core] + alloc_pair[...]
+    alloc_sums[chip] = alloc_chip[chip]
+    send_chips(lambda other: alloc_chip.at[other], alloc_sums, 9)
+
     load_high, load_low = split2(factor_load[...])
     y_high, y_low = split2(weighted[...])
     local = dot(jnp.concatenate([load_high, load_low], axis=0), y_high, NT)
     local = local[:factors] + local[factors:] + dot(load_high, y_low, NT)
-    start_out[...] = local
-    alloc_copy.wait()
-    alloc_chip[...] = alloc_sent[core] + alloc_pair[...]
-    alloc_sums[chip] = alloc_chip[chip]
-    send_chips(lambda other: alloc_chip.at[other], alloc_sums, 9)
+    start_out[...] = DECAY**dates * later_adjoint[...] - DECAY * local
+    start_store = pltpu.make_async_copy(start_out, start_hbm, store_sems.at[0])
+    start_store.start()
 
     wait_chips(rate_sums, recv_sems, 7)
     total = jnp.sum(rate_sums[...], axis=0)
@@ -356,19 +421,32 @@
         jnp.concatenate([total[line : line + 1] for line in range(lines)], axis=1)[:, :grid]
     )
     knot_out[...] = jnp.sum(spline[...] * column, axis=0, keepdims=True)
+    knot_store = pltpu.make_async_copy(knot_out, knot_hbm, store_sems.at[1])
+    knot_store.start()
 
     wait_chips(alloc_sums, recv_sems, 9)
     alloc_out[...] = column_to_row(
         jnp.sum(jnp.sum(alloc_sums[...], axis=0), axis=1, keepdims=True)
     )
+    alloc_store = pltpu.make_async_copy(alloc_out, alloc_hbm, store_sems.at[2])
+    alloc_store.start()
     for buffer, which in ((value_sums, 3), (slope_sums, 5), (rate_sums, 7), (alloc_sums, 9)):
         wait_chips(buffer, send_sems, which)
-
-
-def finish(knot_part, alloc_part, local, later_adjoint, knot_out, alloc_out, start_out, *, dates):
-    knot_out[...] = knot_part[...]
-    alloc_out[...] = alloc_part[...]
-    start_out[...] = DECAY**dates * later_adjoint[...] - DECAY * local[...]
+    for store in (start_store, knot_store, alloc_store):
+        store.wait()
+
+
+def hand_on(knot_part, alloc_part, start_part, knot_out, alloc_out, start_out, sems):
+    copies = []
+    for source, target in (
+        (start_part, start_out),
+        (knot_part, knot_out),
+        (alloc_part, alloc_out),
+    ):
+        copies.append(pltpu.make_async_copy(source, target, sems.at[len(copies)]))
+        copies[-1].start()
+    for copy in copies:
+        copy.wait()
 
 
 def per_device(
@@ -394,7 +472,21 @@
     half = -(-grid // 256) * 128
     lines = -(-grid // 1024) * 8
     vmem = pl.BlockSpec(memory_space=pltpu.VMEM)
-    smem = pl.BlockSpec(memory_space=pltpu.SMEM)
+    hbm = pl.BlockSpec(memory_space=pltpu.HBM)
+    arguments = (
+        trade_set.reshape(1, trades),
+        trade_end.reshape(1, trades),
+        spline_jac,
+        knots.reshape(1, grid),
+        factor_load,
+        vol.reshape(1, dates),
+        start_state,
+        normals,
+        set_cpty.reshape(1, sets),
+        default_prob,
+        base_value,
+        later_adjoint,
+    )
     out_shape = [
         jax.ShapeDtypeStruct((1, grid), F32),
         jax.ShapeDtypeStruct((1, trades), F32),
@@ -403,10 +495,10 @@
     parts = pl.pallas_call(
         functools.partial(kernel, n),
         out_shape=out_shape,
-        in_specs=[smem] * 3 + [vmem] * 4 + [pl.BlockSpec(memory_space=pltpu.HBM)] + [vmem] * 4,
-        out_specs=[vmem] * 3,
-        scratch_shapes=[
-            pltpu.VMEM((grid, grid), F32),
+        in_specs=[vmem] + [hbm] * len(arguments),
+        out_specs=[hbm] * 3,
+        scratch_shapes=[pltpu.VMEM(each.shape, each.dtype) for each in (*arguments, *out_shape)]
+        + [
             pltpu.VMEM((2, n // 2, 2 * trades, half + sets), BF16),
             pltpu.VMEM((2, dates, sets), F32),
             pltpu.VMEM((n // 2, dates, sets), F32),
@@ -422,7 +514,7 @@
             pltpu.VMEM((dates, paths, grid), F32),
             pltpu.VMEM((dates, paths, grid), BF16),
             pltpu.VMEM((dates, paths, sets), F32),
-            pltpu.VMEM((dates * paths, sets), BF16),
+            pltpu.VMEM((dates * paths, sets + 128), BF16),
             pltpu.VMEM((paths, grid), F32),
             pltpu.VMEM((8, grid), F32),
             pltpu.VMEM((dates, grid), F32),
@@ -430,33 +522,24 @@
             pltpu.VMEM((dates, grid), F32),
             pltpu.VMEM((dates, sets), F32),
             pltpu.VMEM((6 * factors, grid), BF16),
-            pltpu.SemaphoreType.DMA,
+            pltpu.VMEM((dates, grid), F32),
+            pltpu.SemaphoreType.DMA((len(arguments),)),
+            pltpu.SemaphoreType.DMA((3,)),
             pltpu.SemaphoreType.DMA((10,)),
             pltpu.SemaphoreType.DMA((10,)),
         ],
         compiler_params=pltpu.CompilerParams(
-            collective_id=0, has_side_effects=True, vmem_limit_bytes=50 * 1024 * 1024
+            collective_id=0, has_side_effects=True, vmem_limit_bytes=58 * 1024 * 1024
         ),
-    )(
-        vol,
-        trade_set.reshape(trades),
-        trade_end,
-        normals,
-        start_state,
-        factor_load,
-        knots.reshape(1, grid),
-        spline_jac,
-        cashflows,
-        set_cpty.reshape(1, sets),
-        default_prob,
-        base_value,
-    )
+    )(cashflows, *arguments)
     knot_grad, alloc, start_adjoint = pl.pallas_call(
-        functools.partial(finish, dates=dates),
+        hand_on,
         out_shape=out_shape,
-        in_specs=[vmem] * 4,
-        out_specs=[vmem] * 3,
-    )(*parts, later_adjoint)
+        in_specs=[hbm] * 3,
+        out_specs=[hbm] * 3,
+        scratch_shapes=[pltpu.SemaphoreType.DMA((3,))],
+        compiler_params=pltpu.CompilerParams(vmem_limit_bytes=58 * 1024 * 1024),
+    )(*parts)
     return knot_grad.reshape(grid), alloc.reshape(trades), start_adjoint
 
 

time: 54.4 us -> 44 us (0.81)
  local copies, waits for them, and re-layouts: 9.77 us -> 0 us
    unnamed x28 -> x0, local copies, waits for them, and re-layouts: 9.77 us -> none
    pallas_call x1, Pallas kernels: 42.1 us -> 40.8 us  [per_device(): pl.pallas_call(functools.partial(kernel, n), out_shape=out_shape, in_spec...]
    pallas_call x1, Pallas kernels: 1.41 us -> 2.26 us  [per_device(): pl.pallas_call(hand_on, out_shape=out_shape, in_specs=[hbm] * 3, out_spec...]
where the time goes in v3:
time: 44 us; the launch traced here: 43.7 us
  Pallas kernels  43.1 us (98%)
  between operations  0.64 us (1%)
    pallas_call x1, Pallas kernels, per_device(): pl.pallas_call(functools.partial(kernel, n), out_shape=out_shape, in_spec...  40.8 us
    pallas_call x1, Pallas kernels, per_device(): pl.pallas_call(hand_on, out_shape=out_shape, in_specs=[hbm] * 3, out_spec...  2.26 us

profile of v3, /device:TPU:0, one launch (start us, length us, event | category | flops | bytes accessed | tf_op | source)
XLA Modules:
  0.0 43.7 jit_solution(6601938833278037147)
XLA Ops:
  0.6 40.8 %shard_map.148 = (f32[1,960]{1,0:T(1,128)}, f32[1,8]{1,0:T(1,128)}, f32[32,256]{1,0:T(8,128)}) custom-call(bf16[8,960]{1,0:T(8,128)(2,1)} %cashflows.1, s32[1,8]{1,0:T(1,128)} %bitcast.8, s32[1,8]{1,0:T(1,128)} %bitcast.9, f32[960,960]{1,0:T(8,128)} %spline_hbm.1, f32[1,960]{1,0:T(1,128)} %bitcast.7, f32[32,960]{1,0:T(8,128)} %factor_load_hbm.1, ...), custom_call_target="tpu_custom_call" | custom-call | tf_op jit(solution)/shard_map/pallas_call | solution.py:495
  41.5 2.3 %shard_map.149 = (f32[1,960]{1,0:T(1,128)}, f32[1,8]{1,0:T(1,128)}, f32[32,256]{1,0:T(8,128)}) custom-call(f32[1,960]{1,0:T(1,128)} %get-tuple-element.9.knot_part, f32[1,8]{1,0:T(1,128)} %get-tuple-element.10.alloc_part, f32[32,256]{1,0:T(8,128)} %get-tuple-element.11.start_part), custom_call_target="tpu_custom_call" | custom-call | tf_op jit(solution)/shard_map/pallas_call | solution.py:535

commit v4 on v3

--- a/solution.py
+++ b/solution.py
@@ -126,6 +126,7 @@
     weight_rows,
     load_split,
     exact_sums,
+    feature_sums,
     load_sems,
     store_sems,
     send_sems,
@@ -250,10 +251,22 @@
     fixing = STEP_YEARS * (date + 1).astype(F32)
     horizon = jnp.where(alive, maturity - fixing, 0.0)
     horizon_rows[...] = horizon
-    loading_rows[...] = (1.0 - jnp.exp(-MEAN_REV * horizon)) / MEAN_REV
+    loading_rows[...] = -((1.0 - jnp.exp(-MEAN_REV * horizon)) / MEAN_REV)
     for load in loads[2:]:
         load.wait()
-    zero_rate = column_to_row(jnp.sum(spline[...] * knots[...], axis=1, keepdims=True))
+    pieces = [slice(first, min(first + 128, grid)) for first in range(0, grid, 128)]
+    zero_rows = []
+    for rows_at in pieces:
+        full = [at for at in pieces if at.stop - at.start == 128]
+        held = spline[rows_at, full[0]] * knots[:, full[0]]
+        for at in full[1:]:
+            held = held + spline[rows_at, at] * knots[:, at]
+        column = jnp.sum(held, axis=1, keepdims=True)
+        if len(full) < len(pieces):
+            at = pieces[-1]
+            column = column + jnp.sum(spline[rows_at, at] * knots[:, at], axis=1, keepdims=True)
+        zero_rows.append(column_to_row(column))
+    zero_rate = jnp.concatenate(zero_rows, axis=1)
     discount_rows[...] = jnp.where(alive, jnp.exp(-zero_rate * horizon), 0.0)
 
     counter = (
@@ -270,14 +283,22 @@
         here = lax.broadcasted_iota(jnp.int32, (1, dates), 1) == i
         date_vol = jnp.sum(jnp.where(here, vol[...], 0.0), axis=1, keepdims=True)
         state = DECAY * state + date_vol * normals[i]
-        s_high, s_mid, s_low = split3(state)
+        s_high, s_mid, s_low = [part.astype(F32) for part in split3(state)]
         stacked = jnp.concatenate([s_high, s_mid, s_high, s_low, s_mid, s_high], axis=0)
-        shift = dot(stacked, load_split[...], TN)
-        bond = jnp.exp(-(loading_rows[pl.ds(i, 1), :] * shift))
-        feat = discount_rows[pl.ds(i, 1), :] * bond
-        exact[i] = feat
-        features[i] = feat.astype(BF16)
-        exact_sums[pl.ds(i, 1), :] = jnp.sum(feat, axis=0, keepdims=True)
+        stacked = stacked.T.astype(BF16)
+        date = pl.ds(i, 1)
+        discount_row, loading_row = discount_rows[date, :], loading_rows[date, :]
+        exact_row, feature_row = [], []
+        for at in pieces:
+            shift = dot(stacked, load_split[:, at], NN)
+            feat = discount_row[:, at] * jnp.exp(loading_row[:, at] * shift)
+            rounded = feat.astype(BF16)
+            exact[i, :, at] = feat
+            features[i, :, at] = rounded
+            exact_row.append(jnp.sum(feat, axis=0, keepdims=True))
+            feature_row.append(jnp.sum(rounded.astype(F32), axis=0, keepdims=True))
+        exact_sums[date, :] = jnp.concatenate(exact_row, axis=1)
+        feature_sums[date, :] = jnp.concatenate(feature_row, axis=1)
         return state
 
     early = dates - dates // 4
@@ -324,12 +345,8 @@
         slope = weights[i : i + 1] * jax.nn.sigmoid(SHARPNESS * shifted)
         total = jnp.sum(slope, axis=0, keepdims=True)
         slope_pair[core, i : i + 1, :] = total
-        adjoint[i * paths : (i + 1) * paths, :sets] = (slope - total / paths).astype(BF16)
+        adjoint[i * paths : (i + 1) * paths, :] = (slope - total / paths).astype(BF16)
     slope_copy = send_pair(slope_pair.at[core], slope_pair.at[core], 4)
-    adjoint[:, sets:] = (
-        lax.broadcasted_iota(jnp.int32, (dates * paths, 128), 0) // paths
-        == lax.broadcasted_iota(jnp.int32, (dates * paths, 128), 1)
-    ).astype(BF16)
     weighted[...] = jnp.zeros_like(weighted)
     rate_acc[...] = jnp.zeros_like(rate_acc)
     loading_rows[...] = loading_rows[...] * jnp.exp(
@@ -338,11 +355,14 @@
     )
 
     def backward(i, carry):
-        adj = adjoint[pl.ds(pl.multiple_of(i * paths, paths), paths), :sets]
-        product = dot(adj, net[...], NN) * exact[i]
-        weighted[...] += loading_rows[pl.ds(i, 1), :] * product
-        folded = jnp.sum(product.reshape(paths // 8, 8, grid), axis=0)
-        rate_acc[...] += horizon_rows[pl.ds(i, 1), :] * folded
+        adj = adjoint[pl.ds(pl.multiple_of(i * paths, paths), paths), :]
+        date = pl.ds(i, 1)
+        loading_row, horizon_row = loading_rows[date, :], horizon_rows[date, :]
+        for at in pieces:
+            product = dot(adj, net[:, at], NN) * exact[i, :, at]
+            weighted[:, at] += loading_row[:, at] * product
+            folded = jnp.sum(product.reshape(paths // 8, 8, at.stop - at.start), axis=0)
+            rate_acc[:, at] += horizon_row[:, at] * folded
         return carry
 
     lax.fori_loop(0, dates // 4, backward, 0)
@@ -373,9 +393,7 @@
             rate_pair[core, line : line + 1, :] = jnp.zeros((1, 128), F32)
     rate_copy = send_pair(rate_pair.at[core], rate_pair.at[core], 6)
 
-    sums = sums[:sets] + dot(
-        remainder, sums[sets : sets + dates], TN, precision=lax.Precision.HIGHEST
-    )
+    sums = sums + dot(remainder, feature_sums[...], TN, precision=lax.Precision.HIGHEST)
     sums = sums * (1.0 / paths_all)
     sums = jnp.concatenate([sums, jnp.zeros((sets, 2 * half - grid), F32)], axis=1)
     stacked = jnp.concatenate(split2(sums), axis=0)
@@ -391,36 +409,37 @@
     send_sum(rate_pair, rate_sums, 7)
 
     loading_rows[...] = loading_rows[...] * common
-    block = 32
-
-    def add_common(step, carry):
-        at = pl.ds(pl.multiple_of(step * block, block), block)
-        held = weighted[at, :]
-        for i in range(dates):
-            held = held + loading_rows[i : i + 1, :] * exact[i, at, :]
-        weighted[at, :] = held
-        return carry
-
-    lax.fori_loop(0, paths // block, add_common, 0)
     alloc_copy.wait()
     alloc_chip[...] = alloc_sent[core] + alloc_pair[...]
     alloc_sums[chip] = alloc_chip[chip]
     send_chips(lambda other: alloc_chip.at[other], alloc_sums, 9)
 
     load_high, load_low = split2(factor_load[...])
-    y_high, y_low = split2(weighted[...])
-    local = dot(jnp.concatenate([load_high, load_low], axis=0), y_high, NT)
-    local = local[:factors] + local[factors:] + dot(load_high, y_low, NT)
-    start_out[...] = DECAY**dates * later_adjoint[...] - DECAY * local
+    load_both = jnp.concatenate([load_high, load_low], axis=0)
+    local = jnp.zeros((factors, paths), F32)
+    for at in pieces:
+        held = weighted[:, at]
+        for i in range(dates):
+            held = held + loading_rows[i : i + 1, at] * exact[i, :, at]
+        y_high, y_low = split2(held)
+        both = dot(load_both[:, at], y_high, NT)
+        local = local + (both[:factors] + both[factors:] + dot(load_high[:, at], y_low, NT))
+    start_out[...] = DECAY**dates * later_adjoint[...] + DECAY * local
     start_store = pltpu.make_async_copy(start_out, start_hbm, store_sems.at[0])
     start_store.start()
 
     wait_chips(rate_sums, recv_sems, 7)
     total = jnp.sum(rate_sums[...], axis=0)
-    column = row_to_column(
-        jnp.concatenate([total[line : line + 1] for line in range(lines)], axis=1)[:, :grid]
-    )
-    knot_out[...] = jnp.sum(spline[...] * column, axis=0, keepdims=True)
+    held = [None] * len(pieces)
+    for line, rows_at in enumerate(pieces):
+        count = rows_at.stop - rows_at.start
+        column = row_to_column(total[line : line + 1, :count])
+        for k, at in enumerate(pieces):
+            product = spline[rows_at, at] * column
+            product = jnp.sum(product.reshape(count // 8, 8, at.stop - at.start), axis=0)
+            held[k] = product if line == 0 else held[k] + product
+    for k, at in enumerate(pieces):
+        knot_out[:, at] = jnp.sum(held[k], axis=0, keepdims=True)
     knot_store = pltpu.make_async_copy(knot_out, knot_hbm, store_sems.at[1])
     knot_store.start()
 
@@ -514,7 +533,7 @@
             pltpu.VMEM((dates, paths, grid), F32),
             pltpu.VMEM((dates, paths, grid), BF16),
             pltpu.VMEM((dates, paths, sets), F32),
-            pltpu.VMEM((dates * paths, sets + 128), BF16),
+            pltpu.VMEM((dates * paths, sets), BF16),
             pltpu.VMEM((paths, grid), F32),
             pltpu.VMEM((8, grid), F32),
             pltpu.VMEM((dates, grid), F32),
@@ -522,6 +541,7 @@
             pltpu.VMEM((dates, grid), F32),
             pltpu.VMEM((dates, sets), F32),
             pltpu.VMEM((6 * factors, grid), BF16),
+            pltpu.VMEM((dates, grid), F32),
             pltpu.VMEM((dates, grid), F32),
             pltpu.SemaphoreType.DMA((len(arguments),)),
             pltpu.SemaphoreType.DMA((3,)),

time: 44 us -> 44 us (level)
  no operation moved by 1% of the time
where the time goes in v4:
time: 44 us; the launch traced here: 43.7 us
  Pallas kernels  43.1 us (98%)
  between operations  0.64 us (1%)
    pallas_call x1, Pallas kernels, per_device(): pl.pallas_call(functools.partial(kernel, n), out_shape=out_shape, in_spec...  40.8 us
    pallas_call x1, Pallas kernels, per_device(): pl.pallas_call(hand_on, out_shape=out_shape, in_specs=[hbm] * 3, out_spec...  2.26 us

profile of v4, /device:TPU:0, one launch (start us, length us, event | category | flops | bytes accessed | tf_op | source)
XLA Modules:
  0.0 43.7 jit_solution(16925869356855887511)
XLA Ops:
  0.6 40.8 %shard_map.148 = (f32[1,960]{1,0:T(1,128)}, f32[1,8]{1,0:T(1,128)}, f32[32,256]{1,0:T(8,128)}) custom-call(bf16[8,960]{1,0:T(8,128)(2,1)} %cashflows.1, s32[1,8]{1,0:T(1,128)} %bitcast.8, s32[1,8]{1,0:T(1,128)} %bitcast.9, f32[960,960]{1,0:T(8,128)} %spline_hbm.1, f32[1,960]{1,0:T(1,128)} %bitcast.7, f32[32,960]{1,0:T(8,128)} %factor_load_hbm.1, ...), custom_call_target="tpu_custom_call" | custom-call | tf_op jit(solution)/shard_map/pallas_call | solution.py:514
  41.5 2.3 %shard_map.149 = (f32[1,960]{1,0:T(1,128)}, f32[1,8]{1,0:T(1,128)}, f32[32,256]{1,0:T(8,128)}) custom-call(f32[1,960]{1,0:T(1,128)} %get-tuple-element.9.knot_part, f32[1,8]{1,0:T(1,128)} %get-tuple-element.10.alloc_part, f32[32,256]{1,0:T(8,128)} %get-tuple-element.11.start_part), custom_call_target="tpu_custom_call" | custom-call | tf_op jit(solution)/shard_map/pallas_call | solution.py:555

commit v5 on v4

--- a/solution.py
+++ b/solution.py
@@ -84,9 +84,9 @@
     default_prob_hbm,
     base_value_hbm,
     later_adjoint_hbm,
-    knot_hbm,
-    alloc_hbm,
-    start_hbm,
+    knot_out,
+    alloc_out,
+    start_out,
     trade_set,
     trade_end,
     spline,
@@ -99,9 +99,6 @@
     default_prob,
     base_value,
     later_adjoint,
-    knot_out,
-    alloc_out,
-    start_out,
     flows,
     value_pair,
     value_sums,
@@ -128,7 +125,6 @@
     exact_sums,
     feature_sums,
     load_sems,
-    store_sems,
     send_sems,
     recv_sems,
 ):
@@ -136,8 +132,9 @@
     grid = knots.shape[1]
     trades = cashflows.shape[0]
     sets = base_value.shape[1]
-    half = flows.shape[3] - sets
+    half = flows.shape[3]
     chips = n // 2
+    short = chips <= 16
     paths_all = paths * n
     me = lax.axis_index("path")
     chip, core = me // 2, me % 2
@@ -169,7 +166,7 @@
         )
         return carry
 
-    lax.fori_loop(1, chips, greet, 0)
+    lax.fori_loop(1, chips, greet, 0, unroll=short)
     pl.semaphore_signal(barrier, inc=1, device_id={"path": partner}, device_id_type=MESH)
 
     loads[0].wait()
@@ -182,17 +179,15 @@
         0.0,
     )
     upper = jnp.concatenate(
-        [live[:, half:], jnp.zeros((trades, 2 * half - grid), F32)], axis=1
-    )
-    one_hot = (lax.broadcasted_iota(jnp.int32, (trades, sets), 1) == set_id).astype(F32)
-    message = jnp.concatenate(
         [
-            jnp.concatenate([live[:, :half], upper], axis=0),
-            jnp.concatenate([one_hot, one_hot], axis=0),
+            live[:, half:],
+            jnp.zeros((trades, 2 * half - grid - 2), F32),
+            (set_id // 128).astype(F32),
+            (set_id % 128).astype(F32),
         ],
         axis=1,
     )
-    flows[core, chip] = message.astype(BF16)
+    flows[core, chip] = jnp.concatenate([live[:, :half], upper], axis=0).astype(BF16)
 
     pl.semaphore_wait(barrier, chips)
 
@@ -207,7 +202,7 @@
         ).start()
         return carry
 
-    lax.fori_loop(1, chips, send_flows, 0)
+    lax.fori_loop(1, chips, send_flows, 0, unroll=short)
 
     def send_pair(buffer, target, which):
         copy = pltpu.make_async_remote_copy(
@@ -234,7 +229,7 @@
             ).start()
             return carry
 
-        lax.fori_loop(1, chips, send, 0)
+        lax.fori_loop(1, chips, send, 0, unroll=short)
 
     def wait_chips(buffer, sems, which):
         others = buffer.at[pl.ds(0, chips - 1)]
@@ -319,10 +314,14 @@
     share.wait()
 
     rows = n * 2 * trades
-    all_flows = flows[:, :, :, :half].reshape(rows, half)
-    member = flows[:, :, :, half:].reshape(rows, sets)
+    all_flows = flows[...].reshape(rows, half)
+    tail = flows[:, :, :, half - 128 :].astype(F32).reshape(n, 2 * trades, 128)
+    tail = tail[:, trades:].reshape(n * trades, 128)
+    all_sets = (128.0 * tail[:, 126:127] + tail[:, 127:128]).astype(jnp.int32)
+    member = lax.broadcasted_iota(jnp.int32, (n * trades, sets), 1) == all_sets
+    member = member.astype(F32).reshape(n, trades, sets)
     is_upper = (lax.broadcasted_iota(jnp.int32, (rows, sets), 0) // trades) % 2 == 1
-    member_wide = member.astype(F32)
+    member_wide = jnp.concatenate([member, member], axis=1).reshape(rows, sets)
     member_low = jnp.where(is_upper, 0.0, member_wide).astype(BF16)
     member_high = jnp.where(is_upper, member_wide, 0.0).astype(BF16)
     net[:, :half] = dot(member_low, all_flows, TN).astype(BF16)
@@ -425,8 +424,6 @@
         both = dot(load_both[:, at], y_high, NT)
         local = local + (both[:factors] + both[factors:] + dot(load_high[:, at], y_low, NT))
     start_out[...] = DECAY**dates * later_adjoint[...] + DECAY * local
-    start_store = pltpu.make_async_copy(start_out, start_hbm, store_sems.at[0])
-    start_store.start()
 
     wait_chips(rate_sums, recv_sems, 7)
     total = jnp.sum(rate_sums[...], axis=0)
@@ -440,19 +437,13 @@
             held[k] = product if line == 0 else held[k] + product
     for k, at in enumerate(pieces):
         knot_out[:, at] = jnp.sum(held[k], axis=0, keepdims=True)
-    knot_store = pltpu.make_async_copy(knot_out, knot_hbm, store_sems.at[1])
-    knot_store.start()
 
     wait_chips(alloc_sums, recv_sems, 9)
     alloc_out[...] = column_to_row(
         jnp.sum(jnp.sum(alloc_sums[...], axis=0), axis=1, keepdims=True)
     )
-    alloc_store = pltpu.make_async_copy(alloc_out, alloc_hbm, store_sems.at[2])
-    alloc_store.start()
     for buffer, which in ((value_sums, 3), (slope_sums, 5), (rate_sums, 7), (alloc_sums, 9)):
         wait_chips(buffer, send_sems, which)
-    for store in (start_store, knot_store, alloc_store):
-        store.wait()
 
 
 def hand_on(knot_part, alloc_part, start_part, knot_out, alloc_out, start_out, sems):
@@ -488,7 +479,7 @@
     grid = knots.shape[0]
     trades = cashflows.shape[0]
     sets = base_value.shape[1]
-    half = -(-grid // 256) * 128
+    half = -(-(grid + 2) // 256) * 128
     lines = -(-grid // 1024) * 8
     vmem = pl.BlockSpec(memory_space=pltpu.VMEM)
     hbm = pl.BlockSpec(memory_space=pltpu.HBM)
@@ -513,12 +504,12 @@
     ]
     parts = pl.pallas_call(
         functools.partial(kernel, n),
-        out_shape=out_shape,
+        out_shape=[pltpu.VMEM(each.shape, each.dtype) for each in out_shape],
         in_specs=[vmem] + [hbm] * len(arguments),
-        out_specs=[hbm] * 3,
-        scratch_shapes=[pltpu.VMEM(each.shape, each.dtype) for each in (*arguments, *out_shape)]
+        out_specs=[vmem] * 3,
+        scratch_shapes=[pltpu.VMEM(each.shape, each.dtype) for each in arguments]
         + [
-            pltpu.VMEM((2, n // 2, 2 * trades, half + sets), BF16),
+            pltpu.VMEM((2, n // 2, 2 * trades, half), BF16),
             pltpu.VMEM((2, dates, sets), F32),
             pltpu.VMEM((n // 2, dates, sets), F32),
             pltpu.VMEM((2, dates, sets), F32),
@@ -544,7 +535,6 @@
             pltpu.VMEM((dates, grid), F32),
             pltpu.VMEM((dates, grid), F32),
             pltpu.SemaphoreType.DMA((len(arguments),)),
-            pltpu.SemaphoreType.DMA((3,)),
             pltpu.SemaphoreType.DMA((10,)),
             pltpu.SemaphoreType.DMA((10,)),
         ],
@@ -555,10 +545,10 @@
     knot_grad, alloc, start_adjoint = pl.pallas_call(
         hand_on,
         out_shape=out_shape,
-        in_specs=[hbm] * 3,
+        in_specs=[vmem] * 3,
         out_specs=[hbm] * 3,
         scratch_shapes=[pltpu.SemaphoreType.DMA((3,))],
-        compiler_params=pltpu.CompilerParams(vmem_limit_bytes=58 * 1024 * 1024),
+        compiler_params=pltpu.CompilerParams(vmem_limit_bytes=1024 * 1024),
     )(*parts)
     return knot_grad.reshape(grid), alloc.reshape(trades), start_adjoint
 

time: 44 us -> 40.4 us (0.918)
  Pallas kernels: 43.1 us -> 39.5 us
    pallas_call x2, Pallas kernels: 43.1 us -> 39.5 us  [the longest x1 38.9 us: per_device(): pl.pallas_call(functools.partial(kernel, n), out_shape=[pltpu.VMEM(each.s...]
where the time goes in v5:
time: 40.4 us; the launch traced here: 40.2 us
  Pallas kernels  39.5 us (98%)
  between operations  0.64 us (2%)
    pallas_call x1, Pallas kernels, per_device(): pl.pallas_call(functools.partial(kernel, n), out_shape=[pltpu.VMEM(each.s...  38.9 us

profile of v5, /device:TPU:0, one launch (start us, length us, event | category | flops | bytes accessed | tf_op | source)
XLA Modules:
  0.0 40.2 jit_solution(2040805469548037074)
XLA Ops:
  0.6 38.9 %shard_map.148 = (f32[1,960]{1,0:T(1,128)S(1)}, f32[1,8]{1,0:T(1,128)S(1)}, f32[32,256]{1,0:T(8,128)S(1)}) custom-call(bf16[8,960]{1,0:T(8,128)(2,1)} %cashflows.1, s32[1,8]{1,0:T(1,128)} %bitcast.8, s32[1,8]{1,0:T(1,128)} %bitcast.9, f32[960,960]{1,0:T(8,128)} %spline_hbm.1, f32[1,960]{1,0:T(1,128)} %bitcast.7, f32[32,960]{1,0:T(8,128)} %factor_load_hbm.1, ...), custom_call_target="tpu_custom_call" | custom-call | tf_op jit(solution)/shard_map/pallas_call | solution.py:505
  39.5 0.6 %shard_map.149 = (f32[1,960]{1,0:T(1,128)}, f32[1,8]{1,0:T(1,128)}, f32[32,256]{1,0:T(8,128)}) custom-call(f32[1,960]{1,0:T(1,128)S(1)} %get-tuple-element.9.knot_part, f32[1,8]{1,0:T(1,128)S(1)} %get-tuple-element.10.alloc_part, f32[32,256]{1,0:T(8,128)S(1)} %get-tuple-element.11.start_part), custom_call_target="tpu_custom_call" | custom-call | tf_op jit(solution)/shard_map/pallas_call | solution.py:545

commit v6 on v5

--- a/solution.py
+++ b/solution.py
@@ -140,6 +140,17 @@
     chip, core = me // 2, me % 2
     partner = me + 1 - 2 * core
 
+    barrier = pltpu.get_barrier_semaphore()
+
+    def greet(step, carry):
+        pl.semaphore_signal(
+            barrier, inc=1, device_id={"path": lax.rem(me + 2 * step, n)}, device_id_type=MESH
+        )
+        return carry
+
+    lax.fori_loop(1, chips, greet, 0, unroll=short)
+    pl.semaphore_signal(barrier, inc=1, device_id={"path": partner}, device_id_type=MESH)
+
     loads = []
     for source, target in (
         (trade_set_hbm, trade_set),
@@ -157,17 +168,6 @@
     ):
         loads.append(pltpu.make_async_copy(source, target, load_sems.at[len(loads)]))
         loads[-1].start()
-
-    barrier = pltpu.get_barrier_semaphore()
-
-    def greet(step, carry):
-        pl.semaphore_signal(
-            barrier, inc=1, device_id={"path": lax.rem(me + 2 * step, n)}, device_id_type=MESH
-        )
-        return carry
-
-    lax.fori_loop(1, chips, greet, 0, unroll=short)
-    pl.semaphore_signal(barrier, inc=1, device_id={"path": partner}, device_id_type=MESH)
 
     loads[0].wait()
     loads[1].wait()
@@ -333,8 +333,15 @@
         value_pair[core, pl.ds(i, 1), :] = jnp.sum(found, axis=0, keepdims=True)
         return carry
 
-    lax.fori_loop(0, dates, value, 0)
-    send_pair(value_pair.at[core], value_pair.at[core], 2).wait()
+    lax.fori_loop(0, dates, value, 0, unroll=True)
+    value_copy = send_pair(value_pair.at[core], value_pair.at[core], 2)
+    weighted[...] = jnp.zeros_like(weighted)
+    rate_acc[...] = jnp.zeros_like(rate_acc)
+    loading_rows[...] = loading_rows[...] * jnp.exp(
+        lax.broadcasted_iota(jnp.int32, (dates, grid), 0).astype(F32)
+        * (-MEAN_REV * STEP_YEARS)
+    )
+    value_copy.wait()
     send_sum(value_pair, value_sums, 3)
     wait_chips(value_sums, recv_sems, 3)
     offset = base_value[...] - jnp.sum(value_sums[...], axis=0) / paths_all
@@ -346,12 +353,6 @@
         slope_pair[core, i : i + 1, :] = total
         adjoint[i * paths : (i + 1) * paths, :] = (slope - total / paths).astype(BF16)
     slope_copy = send_pair(slope_pair.at[core], slope_pair.at[core], 4)
-    weighted[...] = jnp.zeros_like(weighted)
-    rate_acc[...] = jnp.zeros_like(rate_acc)
-    loading_rows[...] = loading_rows[...] * jnp.exp(
-        lax.broadcasted_iota(jnp.int32, (dates, grid), 0).astype(F32)
-        * (-MEAN_REV * STEP_YEARS)
-    )
 
     def backward(i, carry):
         adj = adjoint[pl.ds(pl.multiple_of(i * paths, paths), paths), :]
@@ -364,10 +365,10 @@
             rate_acc[:, at] += horizon_row[:, at] * folded
         return carry
 
-    lax.fori_loop(0, dates // 4, backward, 0)
+    lax.fori_loop(0, dates // 4, backward, 0, unroll=2)
     slope_copy.wait()
     send_sum(slope_pair, slope_sums, 5)
-    lax.fori_loop(dates // 4, dates, backward, 0)
+    lax.fori_loop(dates // 4, dates, backward, 0, unroll=2)
     sums = dot(adjoint[...], features[...].reshape(dates * paths, grid), TN)
 
     wait_chips(slope_sums, recv_sems, 5)
@@ -408,21 +409,27 @@
     send_sum(rate_pair, rate_sums, 7)
 
     loading_rows[...] = loading_rows[...] * common
+    load_high, load_low = split2(factor_load[...])
+    load_both = jnp.concatenate([load_high, load_low], axis=0)
+
+    def last_product(some):
+        local = jnp.zeros((factors, paths), F32)
+        for at in some:
+            held = weighted[:, at]
+            for i in range(dates):
+                held = held + loading_rows[i : i + 1, at] * exact[i, :, at]
+            y_high, y_low = split2(held)
+            both = dot(load_both[:, at], y_high, NT)
+            local = local + (both[:factors] + both[factors:] + dot(load_high[:, at], y_low, NT))
+        return local
+
+    middle = len(pieces) // 2
+    local = last_product(pieces[:middle])
     alloc_copy.wait()
     alloc_chip[...] = alloc_sent[core] + alloc_pair[...]
     alloc_sums[chip] = alloc_chip[chip]
     send_chips(lambda other: alloc_chip.at[other], alloc_sums, 9)
-
-    load_high, load_low = split2(factor_load[...])
-    load_both = jnp.concatenate([load_high, load_low], axis=0)
-    local = jnp.zeros((factors, paths), F32)
-    for at in pieces:
-        held = weighted[:, at]
-        for i in range(dates):
-            held = held + loading_rows[i : i + 1, at] * exact[i, :, at]
-        y_high, y_low = split2(held)
-        both = dot(load_both[:, at], y_high, NT)
-        local = local + (both[:factors] + both[factors:] + dot(load_high[:, at], y_low, NT))
+    local = local + last_product(pieces[middle:])
     start_out[...] = DECAY**dates * later_adjoint[...] + DECAY * local
 
     wait_chips(rate_sums, recv_sems, 7)

time: 40.4 us -> 39.2 us (0.970)
  Pallas kernels: 39.5 us -> 38.3 us
    pallas_call x1, Pallas kernels: 38.9 us -> 37.6 us  [per_device(): pl.pallas_call(functools.partial(kernel, n), out_shape=[pltpu.VMEM(each.s...]
where the time goes in v6:
time: 39.2 us; the launch traced here: 38.9 us
  Pallas kernels  38.3 us (98%)
  between operations  0.64 us (2%)
    pallas_call x1, Pallas kernels, per_device(): pl.pallas_call(functools.partial(kernel, n), out_shape=[pltpu.VMEM(each.s...  37.6 us

profile of v6, /device:TPU:0, one launch (start us, length us, event | category | flops | bytes accessed | tf_op | source)
XLA Modules:
  0.0 38.9 jit_solution(15755741009362470332)
XLA Ops:
  0.6 37.6 %shard_map.148 = (f32[1,960]{1,0:T(1,128)S(1)}, f32[1,8]{1,0:T(1,128)S(1)}, f32[32,256]{1,0:T(8,128)S(1)}) custom-call(bf16[8,960]{1,0:T(8,128)(2,1)} %cashflows.1, s32[1,8]{1,0:T(1,128)} %bitcast.8, s32[1,8]{1,0:T(1,128)} %bitcast.9, f32[960,960]{1,0:T(8,128)} %spline_hbm.1, f32[1,960]{1,0:T(1,128)} %bitcast.7, f32[32,960]{1,0:T(8,128)} %factor_load_hbm.1, ...), custom_call_target="tpu_custom_call" | custom-call | tf_op jit(solution)/shard_map/pallas_call | solution.py:512
  38.3 0.6 %shard_map.149 = (f32[1,960]{1,0:T(1,128)}, f32[1,8]{1,0:T(1,128)}, f32[32,256]{1,0:T(8,128)}) custom-call(f32[1,960]{1,0:T(1,128)S(1)} %get-tuple-element.9.knot_part, f32[1,8]{1,0:T(1,128)S(1)} %get-tuple-element.10.alloc_part, f32[32,256]{1,0:T(8,128)S(1)} %get-tuple-element.11.start_part), custom_call_target="tpu_custom_call" | custom-call | tf_op jit(solution)/shard_map/pallas_call | solution.py:552
